TPU v7x, 128 devices: a whole 4x4x4 slice. The times are simulated.
128 devices in a mesh: row: 16 (over y_hi, z, core), col: 4 (over x), gz: 2 (over y_lo).
Axes of the slice: x: 4, y: 4 (y_hi: 2, y_lo: 2; y = y_hi * 2 + y_lo), z: 4, core: 2. Of those that a mesh axis runs over, the one named last changes fastest.
Arguments:
- velocity_hat: bfloat16 [3, 2, 2, 4096, 4096], P(None, None, 'gz', ('row', 'col')), may hold values from -6 to 6
Outputs:
- smoothed: float32 [2, 4096, 4096], P('gz', 'col', 'row')
All inputs are finite; a program needn't handle non-finite values.
Results may differ from a plain program's by a relative error of at most 0.002.
Values may be sent and summed in bfloat16 or wider, within the bound.
No kernel may reach another device: no remote copies, remote signals or barrier semaphores. Data moves between devices by JAX's collectives and lax.ppermute only.
A program may use at most 128 MiB of HBM per device.

v0:
```python
from functools import partial
import math

import jax
import jax.numpy as jnp
from jax import lax
from jax.sharding import PartitionSpec as P

relax_weight = 0.15
contract = partial(jnp.einsum, precision=lax.Precision.HIGHEST, preferred_element_type=jnp.float32)


def passed_along(value, axis, steps):
    count = lax.axis_size(axis)
    pairs = [(source, (source + steps) % count) for source in range(count)]
    return lax.ppermute(value, axis, pairs)


def shortened(array):

    def short(part):
        return part.astype(jnp.bfloat16) if part.dtype == jnp.float32 else part

    return jax.tree.map(short, array)


def with_halo(block, sides, width):
    for axis, dim in sides:
        count = lax.axis_size(axis)
        forward = [(i, i + 1) for i in range(count - 1)]
        forward.append((count - 1, 0))
        backward = [(target, source) for source, target in forward]
        low = lax.ppermute(
            lax.slice_in_dim(block, block.shape[dim] - width, None, axis=dim), axis, forward
        )
        high = lax.ppermute(lax.slice_in_dim(block, 0, width, axis=dim), axis, backward)
        block = jnp.concatenate([low, block, high], axis=dim)
    return block


def wavenumber(index, length):
    signed = (index + length // 2) % length - length // 2
    return signed.astype(jnp.float32) * (2.0 * math.pi / length)


def phase_table(rows_len, cols_len, modulus):
    product = lax.broadcasted_iota(jnp.int32, (rows_len, cols_len), 0) * lax.broadcasted_iota(
        jnp.int32, (rows_len, cols_len), 1
    )
    angle = (product % modulus).astype(jnp.float32) * (2.0 * math.pi / modulus)
    return (jnp.cos(angle), jnp.sin(angle))


def inverse_transform(real_part, imag_part, on_last, keep_imag):
    length = real_part.shape[-1] if on_last else real_part.shape[-2]
    lead_dims = real_part.shape[:-1] if on_last else real_part.shape[:-2]
    tail_dims = () if on_last else real_part.shape[-1:]
    inner_len = 1 << (length.bit_length() - 1) // 2
    outer_len = length // inner_len
    split_shape = lead_dims + (outer_len, inner_len) + tail_dims
    first_real = real_part.reshape(split_shape)
    first_imag = imag_part.reshape(split_shape)
    letter = "" if on_last else "m"
    cos_outer, sin_outer = phase_table(outer_len, outer_len, outer_len)
    spec_one = "...qk" + letter + ",qn->...nk" + letter
    mid_real = contract(spec_one, first_real, cos_outer) - contract(spec_one, first_imag, sin_outer)
    mid_imag = contract(spec_one, first_real, sin_outer) + contract(spec_one, first_imag, cos_outer)
    twist_cos, twist_sin = phase_table(outer_len, inner_len, length)
    if not on_last:
        twist_cos = twist_cos[:, :, None]
        twist_sin = twist_sin[:, :, None]
    turned_real = mid_real * twist_cos - mid_imag * twist_sin
    turned_imag = mid_real * twist_sin + mid_imag * twist_cos
    cos_inner, sin_inner = phase_table(inner_len, inner_len, inner_len)
    spec_two = "...nk" + letter + ",kp->...pn" + letter
    factor_norm = 1.0 / math.sqrt(length)
    out_shape = lead_dims + (length,) + tail_dims
    out_real = (
        (contract(spec_two, turned_real, cos_inner) - contract(spec_two, turned_imag, sin_inner))
        * factor_norm
    ).reshape(out_shape)
    if not keep_imag:
        return out_real
    out_imag = (
        (contract(spec_two, turned_real, sin_inner) + contract(spec_two, turned_imag, cos_inner))
        * factor_norm
    ).reshape(out_shape)
    return (out_real, out_imag)


def relax_core(padded):
    center = padded[1:-1, 1:-1, 1:-1]
    beside_all = padded[:-2, 1:-1, 1:-1] + padded[2:, 1:-1, 1:-1]
    beside_all = beside_all + padded[1:-1, :-2, 1:-1] + padded[1:-1, 2:, 1:-1]
    beside_all = beside_all + padded[1:-1, 1:-1, :-2] + padded[1:-1, 1:-1, 2:]
    return center + relax_weight * (beside_all - 6.0 * center)


def along_y(block):
    return inverse_transform(block[:, 0], block[:, 1], False, False)


def shards(velocity_hat):
    rows_local = velocity_hat.shape[3]
    grid_len = velocity_hat.shape[4]
    first_plane = velocity_hat[0:2, :, 0:1]
    next_first = passed_along(first_plane, "gz", -1)
    above = jnp.concatenate([velocity_hat[0:2, :, 1:], next_first], axis=2)
    parts = velocity_hat.astype(jnp.float32)
    plane_diff = above.astype(jnp.float32) - parts[0:2]
    wave_x = wavenumber(jnp.arange(grid_len, dtype=jnp.int32), grid_len)[None, None, :]
    row_start = lax.axis_index(("row", "col")) * rows_local
    wave_y = wavenumber(row_start + jnp.arange(rows_local, dtype=jnp.int32), grid_len)[
        None, :, None
    ]
    vel_x_re, vel_x_im = (parts[0, 0], parts[0, 1])
    vel_y_re, vel_y_im = (parts[1, 0], parts[1, 1])
    vel_z_re, vel_z_im = (parts[2, 0], parts[2, 1])
    curl_real = jnp.stack(
        [
            -wave_y * vel_z_im - plane_diff[1, 0],
            plane_diff[0, 0] + wave_x * vel_z_im,
            -(wave_x * vel_y_im - wave_y * vel_x_im),
        ]
    )
    curl_imag = jnp.stack(
        [
            wave_y * vel_z_re - plane_diff[1, 1],
            plane_diff[0, 1] - wave_x * vel_z_re,
            wave_x * vel_y_re - wave_y * vel_x_re,
        ]
    )
    line_real, line_imag = inverse_transform(curl_real, curl_imag, True, True)
    spectral_x = jnp.stack([line_real, line_imag], axis=1)
    vort = along_y(
        lax.all_to_all(
            shortened(spectral_x), ("row", "col"), split_axis=4, concat_axis=3, tiled=True
        ).astype(spectral_x.dtype)
    )
    total = 1.0 + vort[0] * vort[0] + vort[1] * vort[1] + vort[2] * vort[2]
    magnitude = jnp.sqrt(total)
    field = lax.all_to_all(
        shortened(magnitude), "col", split_axis=1, concat_axis=2, tiled=True
    ).astype(magnitude.dtype)
    for pass_index in range(3):
        padded = with_halo(field, (("row", 2), ("col", 1), ("gz", 0)), 1)
        field = relax_core(padded)
    return field


def solution(mesh):
    return jax.shard_map(
        shards,
        mesh=mesh,
        in_specs=(P(None, None, "gz", ("row", "col"), None),),
        out_specs=P("gz", "col", "row"),
        check_vma=False,
    )
```

profile of v0, /device:TPU:0, one launch (start us, length us, event | category | flops | bytes accessed | tf_op | source)
XLA Modules:
  0.0 671.7 jit_solution(9549839112434501400)
XLA Ops:
  26.8 24.2 %collective-permute-done = bf16[2,2,1,64,4096]{4,3,2,1,0:T(8,128)(2,1)} collective-permute-done((bf16[2,2,1,64,4096]{4,3,2,1,0:T(8,128)(2,1)}, bf16[2,2,1,64,4096]{4,3,2,1,0:T(8,128)(2,1)}, u32[]{:S(2)}, u32[]{:S(2)}) %collective-permute-start) | collective-permute-done | bytes 2097184 | tf_op jit(solution)/shard_map/ppermute | solution.py:16
  60.0 7.2 %multiply_subtract_fusion.2 = (f32[1,1,64,64,64]{4,3,2,0,1:T(8,128)S(1)}, f32[1,1,64,64,64]{4,3,2,0,1:T(8,128)S(1)}, f32[1,1,64,64,64]{4,3,2,0,1:T(8,128)S(1)}, f32[1,1,64,64,64]{4,3,2,0,1:T(8,128)S(1)}) fusion(f32[1,1,64,64,64]{4,3,2,0,1:T(8,128)} %squeeze.42, f32[1,1,64,64,64]{4,3,2,0,1:T(8,128)} %squeeze.41, f32[64]{0:T(128)S(1)} %get-tuple-element.39, ...), kind=kLoop, calls=%fused_computation.50 | loop fusion | flops 2883584 | bytes 11550976 | tf_op jit(solution)/shard_map/sub | solution.py:128
  67.2 8.0 %fusion.19 = f32[64,3,64,64]{3,0,2,1:T(8,128)} fusion(f32[1,1,64,64,64]{4,3,2,0,1:T(8,128)S(1)} %get-tuple-element.37, f32[1,1,64,64,64]{4,3,2,0,1:T(8,128)S(1)} %get-tuple-element.22, f32[1,1,64,64,64]{4,3,2,0,1:T(8,128)S(1)} %get-tuple-element.21), kind=kOutput, calls=%fused_computation.34 | convolution fusion | flops 605609984 | bytes 6291456 | tf_op jit(solution)/shard_map/...qk,qn->...nk/dot_general | solution.py:66
  75.2 7.7 %fusion.18 = f32[64,3,64,64]{3,0,2,1:T(8,128)} fusion(f32[1,1,64,64,64]{4,3,2,0,1:T(8,128)S(1)} %get-tuple-element.37, f32[1,1,64,64,64]{4,3,2,0,1:T(8,128)S(1)} %get-tuple-element.22, f32[1,1,64,64,64]{4,3,2,0,1:T(8,128)S(1)} %get-tuple-element.21), kind=kOutput, calls=%fused_computation.33 | convolution fusion | flops 605609984 | bytes 6291456 | tf_op jit(solution)/shard_map/...qk,qn->...nk/dot_general | solution.py:67
  93.3 7.8 %fusion.21 = f32[64,3,64,64]{3,0,2,1:T(8,128)} fusion(f32[1,1,64,64,64]{4,3,2,0,1:T(8,128)S(1)} %get-tuple-element.38, f32[1,1,64,64,64]{4,3,2,0,1:T(8,128)S(1)} %get-tuple-element.24, f32[1,1,64,64,64]{4,3,2,0,1:T(8,128)S(1)} %get-tuple-element.23), kind=kOutput, calls=%fused_computation.36 | convolution fusion | flops 605609984 | bytes 6291456 | tf_op jit(solution)/shard_map/...qk,qn->...nk/dot_general | solution.py:66
  101.1 13.0 %fusion.12 = (f32[64,3,1,64,64]{4,0,3,1,2:T(8,128)S(1)}, f32[64,3,1,64,64]{4,0,3,1,2:T(8,128)S(1)}) fusion(f32[64,64]{1,0:T(8,128)S(1)} %copy.66, f32[64,64]{1,0:T(8,128)S(1)} %copy.65, f32[64,3,64,64]{3,0,2,1:T(8,128)} %fusion.18, f32[64,3,64,64]{3,0,2,1:T(8,128)} %fusion.21, f32[64,3,64,64]{3,0,2,1:T(8,128)} %fusion.19, ...), kind=kOutput, calls=%fused_computation.22 | convolution fusion | flops 611901440 | bytes 18907136 | tf_op jit(solution)/shard_map/...qk,qn->...nk/dot_general | solution.py:67
  114.1 18.2 %fusion.6 = f32[64,3,64,64]{3,0,2,1:T(8,128)S(1)} fusion(f32[64,3,1,64,64]{4,0,3,1,2:T(8,128)S(1)} %get-tuple-element.8), kind=kOutput, calls=%fused_computation.14 | convolution fusion | flops 604037120 | bytes 6291456 | tf_op jit(solution)/shard_map/...nk,kp->...pn/dot_general | solution.py:79
  132.3 20.2 %fusion.4 = f32[64,3,64,64]{3,0,2,1:T(8,128)} fusion(f32[64,3,1,64,64]{4,0,3,1,2:T(8,128)S(1)} %get-tuple-element.8), kind=kOutput, calls=%fused_computation.12 | convolution fusion | flops 604037120 | bytes 6291456 | tf_op jit(solution)/shard_map/...nk,kp->...pn/dot_general | solution.py:85
  152.5 18.3 %fusion.22 = bf16[3,1,64,64,64]{4,3,2,0,1:T(8,128)(2,1)S(1)} fusion(f32[64,3,64,64]{3,0,2,1:T(8,128)S(1)} %fusion.6, f32[64,3,1,64,64]{4,0,3,1,2:T(8,128)S(1)} %get-tuple-element.7), kind=kOutput, calls=%fused_computation.38 | convolution fusion | flops 606396416 | bytes 7864320 | tf_op jit(solution)/shard_map/...nk,kp->...pn/dot_general | solution.py:79
  174.3 14.1 %copy.67 = bf16[3,1,1,64,4096]{3,1,0,2,4:T(2,128)(2,1)} copy(bf16[3,1,1,64,4096]{4,3,0,2,1:T(8,128)(2,1)} %stack.21) | data formatting | bytes 3145728 | tf_op jit(solution)/shard_map/stack | solution.py:134
  188.5 21.4 %fusion.23 = bf16[3,1,64,64,64]{4,3,2,0,1:T(8,128)(2,1)S(1)} fusion(f32[64,3,64,64]{3,0,2,1:T(8,128)} %fusion.4, f32[64,3,1,64,64]{4,0,3,1,2:T(8,128)} %copy-done), kind=kOutput, calls=%fused_computation.39 | convolution fusion | flops 606396416 | bytes 7864320 | tf_op jit(solution)/shard_map/...nk,kp->...pn/dot_general | solution.py:85
  213.3 14.2 %copy.68 = bf16[3,1,1,64,4096]{3,1,0,2,4:T(2,128)(2,1)} copy(bf16[3,1,1,64,4096]{4,3,0,2,1:T(8,128)(2,1)} %stack.22) | data formatting | bytes 3145728 | tf_op jit(solution)/shard_map/stack | solution.py:134
  227.6 19.1 %fusion.181 = bf16[4096,1,3,2,64]{4,3,2,1,0:T(2,128)(2,1)} fusion(bf16[3,1,1,64,4096]{3,1,0,2,4:T(2,128)(2,1)} %copy.68, bf16[3,1,1,64,4096]{3,1,0,2,4:T(2,128)(2,1)} %copy.67), kind=kLoop, calls=%fused_computation.228 | loop fusion | flops 6291456 | bytes 6291456
  246.7 13.1 %reshape.593 = bf16[64,2,12288]{2,1,0:T(2,128)(2,1)S(1)} reshape(bf16[4096,1,3,2,64]{4,3,2,1,0:T(2,128)(2,1)} %fusion.181) | data formatting | bytes 6291456
  259.8 54.3 %all_to_all.27 = bf16[64,2,12288]{2,1,0:T(2,128)(2,1)} all-to-all(bf16[64,2,12288]{2,1,0:T(2,128)(2,1)S(1)} %reshape.593), channel_id=1, replica_groups=mesh['row'=16,'col'=4,'gz'=2] {'row','col'}, dimensions={0} | all-to-all | bytes 6291456 | tf_op jit(solution)/shard_map/all_to_all | solution.py:136
  314.0 13.8 %reshape.594 = bf16[4096,1,3,2,64]{4,3,2,1,0:T(2,128)(2,1)} reshape(bf16[64,2,12288]{2,1,0:T(2,128)(2,1)} %all_to_all.27) | data formatting | bytes 6291456
  327.9 9.5 %copy.125 = bf16[3,2,1,64,64,64]{3,4,5,1,0,2:T(8,128)(2,1)} copy(bf16[3,2,1,64,64,64]{3,1,0,5,4,2:T(2,128)(2,1)} %bitcast.178) | data formatting | bytes 6291456 | tf_op jit(solution)/shard_map/all_to_all | solution.py:136
  337.3 7.9 %all_to_all.23 = bf16[3,2,1,4096,64]{3,4,1,0,2:T(8,128)(2,1)S(1)} reshape(bf16[3,2,1,64,64,64]{4,3,5,1,0,2:T(8,128)(2,1)} %bitcast.179) | data formatting | bytes 6291456 | tf_op jit(solution)/shard_map/all_to_all | solution.py:136
  352.6 5.8 copy.72
  373.4 5.8 copy.71
  381.9 10.0 %fusion.1 = (f32[3,64,64,64]{3,1,2,0:T(8,128)}, f32[3,64,64,64]{3,1,2,0:T(8,128)S(1)}) fusion(f32[64,64]{0,1:T(8,128)S(1)} %get-tuple-element.41, f32[64,64]{0,1:T(8,128)S(1)} %get-tuple-element.42, f32[64,3,64,64]{3,0,2,1:T(8,128)S(1)} %fusion.65, f32[64,3,64,64]{3,0,2,1:T(8,128)} %fusion.74, f32[64,3,64,64]{3,0,2,1:T(8,128)} %fusion.67, ...), kind=kOutput, calls=%fused_computation.6 | convolution fusion | flops 610328576 | bytes 17334272 | tf_op jit(solution)/shard_map/...qkm,qn->...nkm/dot_general | solution.py:66
  392.0 9.5 %fusion.14 = f32[64,3,64,64]{3,0,2,1:T(8,128)S(1)} fusion(f32[3,64,64,64]{3,1,2,0:T(8,128)S(1)} %get-tuple-element.6), kind=kOutput, calls=%fused_computation.26 | convolution fusion | flops 604037120 | bytes 6291456 | tf_op jit(solution)/shard_map/...nkm,kp->...pnm/dot_general | solution.py:79
  401.5 10.6 %multiply_bitcast_fusion = f32[3,1,64,64,64]{4,2,3,0,1:T(8,128)S(1)} fusion(f32[64,3,64,64]{3,0,2,1:T(8,128)S(1)} %fusion.14, f32[3,64,64,64]{3,1,2,0:T(8,128)S(1)} %copy-done.2), kind=kOutput, calls=%fused_computation.30 | convolution fusion | flops 605609984 | bytes 9437184 | tf_op jit(solution)/shard_map/...nkm,kp->...pnm/dot_general | solution.py:79
  414.8 22.6 %reduce = bf16[4096,64]{1,0:T(8,128)(2,1)S(1)} reduce(bf16[4096,1,64]{2,1,0:T(2,128)(2,1)S(1)} %bitcast.184, bf16[]{:T(256)} %broadcast.505), dimensions={1}, to_apply=%bitcast.164.reduce_sub_computation | reduce | bytes 1048578
  438.2 12.2 %all_to_all.28 = bf16[4,2,32768]{2,1,0:T(2,128)(2,1)S(1)} all-to-all(bf16[4,2,32768]{2,1,0:T(2,128)(2,1)S(1)} %reshape.595), channel_id=1, replica_groups=mesh['row'=16,'col'=4,'gz'=2] {'col'}, dimensions={0} | all-to-all | bytes 1048576 | tf_op jit(solution)/shard_map/all_to_all | solution.py:142
  474.9 26.9 %collective-permute-done.5 = f32[1,1026,258]{1,0,2:T(1,128)S(1)} collective-permute-done((f32[1,1026,258]{1,0,2:T(1,128)S(1)}, f32[1,1026,258]{1,0,2:T(1,128)S(1)}, u32[]{:S(2)}, u32[]{:S(2)}) %collective-permute-start.5) | collective-permute-done | bytes 1058864 | tf_op jit(solution)/shard_map/ppermute | solution.py:33
  504.0 18.0 %collective-permute-done.6 = f32[1,1026,258]{1,0,2:T(1,128)S(1)} collective-permute-done((f32[1,1026,258]{1,0,2:T(1,128)S(1)}, f32[1,1026,258]{1,0,2:T(1,128)S(1)}, u32[]{:S(2)}, u32[]{:S(2)}) %collective-permute-start.6) | collective-permute-done | bytes 1058864 | tf_op jit(solution)/shard_map/ppermute | solution.py:36
  547.1 26.7 %collective-permute-done.11 = f32[1,1026,258]{1,0,2:T(1,128)S(1)} collective-permute-done((f32[1,1026,258]{1,0,2:T(1,128)S(1)}, f32[1,1026,258]{1,0,2:T(1,128)S(1)}, u32[]{:S(2)}, u32[]{:S(2)}) %collective-permute-start.11) | collective-permute-done | bytes 1058864 | tf_op jit(solution)/shard_map/ppermute | solution.py:33
  576.0 16.6 %collective-permute-done.12 = f32[1,1026,258]{1,0,2:T(1,128)S(1)} collective-permute-done((f32[1,1026,258]{1,0,2:T(1,128)S(1)}, f32[1,1026,258]{1,0,2:T(1,128)S(1)}, u32[]{:S(2)}, u32[]{:S(2)}) %collective-permute-start.12) | collective-permute-done | bytes 1058864 | tf_op jit(solution)/shard_map/ppermute | solution.py:36
  597.0 5.8 collective-permute-start.14
  617.2 26.9 %collective-permute-done.17 = f32[1,1026,258]{1,0,2:T(1,128)S(1)} collective-permute-done((f32[1,1026,258]{1,0,2:T(1,128)S(1)}, f32[1,1026,258]{1,0,2:T(1,128)S(1)}, u32[]{:S(2)}, u32[]{:S(2)}) %collective-permute-start.17) | collective-permute-done | bytes 1058864 | tf_op jit(solution)/shard_map/ppermute | solution.py:33
  646.3 20.5 %collective-permute-done.18 = f32[1,1026,258]{1,0,2:T(1,128)S(1)} collective-permute-done((f32[1,1026,258]{1,0,2:T(1,128)S(1)}, f32[1,1026,258]{1,0,2:T(1,128)S(1)}, u32[]{:S(2)}, u32[]{:S(2)}) %collective-permute-start.18) | collective-permute-done | bytes 1058864 | tf_op jit(solution)/shard_map/ppermute | solution.py:36
  (104 shorter events, 161.3 us)
Async XLA Ops:
  0.0 5.0 copy-start.1
  3.4 47.6 %collective-permute-start = (bf16[2,2,1,64,4096]{4,3,2,1,0:T(8,128)(2,1)}, bf16[2,2,1,64,4096]{4,3,2,1,0:T(8,128)(2,1)}, u32[]{:S(2)}, u32[]{:S(2)}) collective-permute-start(bf16[2,2,1,64,4096]{4,3,2,1,0:T(8,128)(2,1)} %slice.160), channel_id=1, source_target_pairs={{0,1},{1,0},{2,3},{3,2},{4,5},{5,4},{6,7},{7,6},{8,9},{9,8},{10,11... | collective-permute-start | bytes 6291464 | tf_op jit(solution)/shard_map/ppermute | solution.py:16
  91.3 1.4 copy-start.3
  91.3 2.0 copy-start.4
  114.1 38.4 %copy-start = (f32[64,3,1,64,64]{4,0,3,1,2:T(8,128)}, f32[64,3,1,64,64]{4,0,3,1,2:T(8,128)S(1)}, u32[]{:S(2)}) copy-start(f32[64,3,1,64,64]{4,0,3,1,2:T(8,128)S(1)} %get-tuple-element.7) | copy-start | bytes 9437188
  392.0 9.5 %copy-start.2 = (f32[3,64,64,64]{3,1,2,0:T(8,128)S(1)}, f32[3,64,64,64]{3,1,2,0:T(8,128)}, u32[]{:S(2)}) copy-start(f32[3,64,64,64]{3,1,2,0:T(8,128)} %get-tuple-element.5) | copy-start | bytes 9437188
  455.1 6.7 collective-permute-start.1
  455.2 6.7 collective-permute-start.2
  462.1 6.3 collective-permute-start.3
  462.7 5.7 collective-permute-start.4
  472.6 29.2 %collective-permute-start.5 = (f32[1,1026,258]{1,0,2:T(1,128)S(1)}, f32[1,1026,258]{1,0,2:T(1,128)S(1)}, u32[]{:S(2)}, u32[]{:S(2)}) collective-permute-start(f32[1,1026,258]{1,0,2:T(1,128)S(1)} %copy.81), channel_id=1, source_target_pairs={{0,1},{1,0},{2,3},{3,2},{4,5},{5,4},{6,7},{7,6},{8,9},{9,8},{10,11... | collective-permute-start | bytes 3176504 | tf_op jit(solution)/shard_map/ppermute | solution.py:33
  473.4 48.7 %collective-permute-start.6 = (f32[1,1026,258]{1,0,2:T(1,128)S(1)}, f32[1,1026,258]{1,0,2:T(1,128)S(1)}, u32[]{:S(2)}, u32[]{:S(2)}) collective-permute-start(f32[1,1026,258]{1,0,2:T(1,128)S(1)} %copy.81), channel_id=1, source_target_pairs={{1,0},{0,1},{3,2},{2,3},{5,4},{4,5},{7,6},{6,7},{9,8},{8,9},{11,10... | collective-permute-start | bytes 3176504 | tf_op jit(solution)/shard_map/ppermute | solution.py:36
  525.5 6.7 collective-permute-start.7
  525.6 6.7 collective-permute-start.8
  532.5 5.6 collective-permute-start.10
  535.5 6.3 collective-permute-start.9
  544.6 29.2 %collective-permute-start.11 = (f32[1,1026,258]{1,0,2:T(1,128)S(1)}, f32[1,1026,258]{1,0,2:T(1,128)S(1)}, u32[]{:S(2)}, u32[]{:S(2)}) collective-permute-start(f32[1,1026,258]{1,0,2:T(1,128)S(1)} %copy.85), channel_id=1, source_target_pairs={{0,1},{1,0},{2,3},{3,2},{4,5},{5,4},{6,7},{7,6},{8,9},{9,8},{10,11... | collective-permute-start | bytes 3176504 | tf_op jit(solution)/shard_map/ppermute | solution.py:33
  545.4 47.3 %collective-permute-start.12 = (f32[1,1026,258]{1,0,2:T(1,128)S(1)}, f32[1,1026,258]{1,0,2:T(1,128)S(1)}, u32[]{:S(2)}, u32[]{:S(2)}) collective-permute-start(f32[1,1026,258]{1,0,2:T(1,128)S(1)} %copy.85), channel_id=1, source_target_pairs={{1,0},{0,1},{3,2},{2,3},{5,4},{4,5},{7,6},{6,7},{9,8},{8,9},{11,10... | collective-permute-start | bytes 3176504 | tf_op jit(solution)/shard_map/ppermute | solution.py:36
  597.0 7.1 %collective-permute-start.13 = (f32[1,1024,1]{1,2,0:T(1,128)S(1)}, f32[1,1024,1]{1,2,0:T(1,128)S(1)}, u32[]{:S(2)}, u32[]{:S(2)}) collective-permute-start(f32[1,1024,1]{1,2,0:T(1,128)S(1)} %get-tuple-element.31), channel_id=1, source_target_pairs={{0,8},{8,16},{16,24},{24,32},{32,40},{40,48},{48,56},{56,64},{64,7... | collective-permute-start | bytes 12296 | tf_op jit(solution)/shard_map/ppermute | solution.py:33
  597.0 7.1 %collective-permute-start.14 = (f32[1,1024,1]{1,2,0:T(1,128)S(1)}, f32[1,1024,1]{1,2,0:T(1,128)S(1)}, u32[]{:S(2)}, u32[]{:S(2)}) collective-permute-start(f32[1,1024,1]{1,2,0:T(1,128)S(1)} %get-tuple-element.32), channel_id=1, source_target_pairs={{8,0},{16,8},{24,16},{32,24},{40,32},{48,40},{56,48},{64,56},{72,6... | collective-permute-start | bytes 12296 | tf_op jit(solution)/shard_map/ppermute | solution.py:36
  604.4 6.3 collective-permute-start.15
  604.5 6.2 collective-permute-start.16
  614.9 29.2 %collective-permute-start.17 = (f32[1,1026,258]{1,0,2:T(1,128)S(1)}, f32[1,1026,258]{1,0,2:T(1,128)S(1)}, u32[]{:S(2)}, u32[]{:S(2)}) collective-permute-start(f32[1,1026,258]{1,0,2:T(1,128)S(1)} %copy.89), channel_id=1, source_target_pairs={{0,1},{1,0},{2,3},{3,2},{4,5},{5,4},{6,7},{7,6},{8,9},{9,8},{10,11... | collective-permute-start | bytes 3176504 | tf_op jit(solution)/shard_map/ppermute | solution.py:33
  616.3 50.5 %collective-permute-start.18 = (f32[1,1026,258]{1,0,2:T(1,128)S(1)}, f32[1,1026,258]{1,0,2:T(1,128)S(1)}, u32[]{:S(2)}, u32[]{:S(2)}) collective-permute-start(f32[1,1026,258]{1,0,2:T(1,128)S(1)} %copy.89), channel_id=1, source_target_pairs={{1,0},{0,1},{3,2},{2,3},{5,4},{4,5},{7,6},{6,7},{9,8},{8,9},{11,10... | collective-permute-start | bytes 3176504 | tf_op jit(solution)/shard_map/ppermute | solution.py:36
where the time goes:
time: 682 us; the launch traced here: 672 us
  waiting for transfers between devices  176 us (26%)
  local copies, waits for them, and re-layouts  172 us (25%)
  matrix products  157 us (23%)
  blocking collectives  66.5 us (10%)
  other arithmetic  64.9 us (10%)
  starting transfers between devices  35 us (5%)
    ppermute x9, waiting for transfers between devices, with_halo(): lax.ppermute(lax.slice_in_dim(block, block.shape[dim] - width, None, axis...  94 us
    ppermute x9, waiting for transfers between devices, with_halo(): lax.ppermute(lax.slice_in_dim(block, 0, width, axis=dim), axis, backward)  57.9 us
    all_to_all x1, blocking collectives, shards(): lax.all_to_all(shortened(spectral_x), ('row', 'col'), split_axis=4, conca...  54.3 us
    unnamed x2, other arithmetic  41.7 us
    another operation x4, local copies, waits for them, and re-layouts, shards(): spectral_x = jnp.stack([line_real, line_imag], axis=1)  35.3 us
    unnamed x15, local copies, waits for them, and re-layouts  31.2 us
    ppermute x9, starting transfers between devices, with_halo(): lax.ppermute(lax.slice_in_dim(block, 0, width, axis=dim), axis, backward)  29.5 us
    dot_general x2, matrix products, inverse_transform(): contract(spec_two, turned_real, cos_inner)  29 us
  transfers between devices with their start and end apart: 19, of which 15 were waited for; matrix products, arithmetic and copies ran while one was open for 4% of the time, Pallas kernels for 0%

commit v1 on v0

v1 whole, which is shorter than its diff:
```python
import math

import jax
import jax.numpy as jnp
import numpy as np
from jax import lax
from jax.experimental import pallas as pl
from jax.experimental.pallas import tpu as pltpu
from jax.sharding import PartitionSpec as P

GRID = 4096
RELAX = 0.15
VMEM_LIMIT = 48 * 1024 * 1024
NT = (((1,), (1,)), ((), ()))


def split_bf16(table):
    high = table.astype(jnp.bfloat16)
    low = (table - high.astype(np.float64)).astype(jnp.bfloat16)
    return np.concatenate([high, low], axis=0)


def tables():
    k = np.arange(128)
    blocks = []
    for s in range(2):
        angle = 2 * np.pi * ((np.arange(64)[:, None] * 2 + s) * k[None, :] % 128) / 128
        c, d = np.cos(angle), np.sin(angle)
        blocks.append(np.concatenate([c, -d], axis=1))
        blocks.append(np.concatenate([d, c], axis=1))
    x_matrix = split_bf16(np.concatenate(blocks, axis=0))
    angle = 2 * np.pi * (np.arange(32)[:, None] * k[None, :]) / 4096
    x_twist = np.stack([np.cos(angle), np.sin(angle)]).astype(np.float32) / 64
    j = np.arange(64)
    angle = 2 * np.pi * (j[:, None] * j[None, :] % 64) / 64
    zero = np.zeros((64, 64))
    c, d = np.cos(angle), -np.sin(angle)
    y_matrix = split_bf16(
        np.concatenate(
            [np.concatenate([c, zero, d, zero], axis=1), np.concatenate([zero, c, zero, d], axis=1)], axis=0
        )
    )
    angle = 2 * np.pi * (j[:, None] * j[None, :]) / 4096
    y_twist = np.stack([np.cos(angle), np.sin(angle)]).astype(np.float32) / 64
    y_twist = np.concatenate([y_twist, y_twist], axis=2)
    return x_matrix, x_twist, y_matrix, y_twist


def turned(value, num, den):
    re, im = value
    num = num % den
    if num == 0:
        return value
    if 2 * num == den:
        return (-re, -im)
    if 4 * num == den:
        return (-im, re)
    if 4 * num == 3 * den:
        return (im, -re)
    if 8 * num == den:
        r = math.sqrt(0.5)
        return ((re - im) * r, (re + im) * r)
    if 8 * num == 3 * den:
        r = math.sqrt(0.5)
        return ((re + im) * -r, (re - im) * r)
    c, s = math.cos(2 * math.pi * num / den), math.sin(2 * math.pi * num / den)
    return (re * c - im * s, re * s + im * c)


def plus(a, b):
    return (a[0] + b[0], a[1] + b[1])


def minus(a, b):
    return (a[0] - b[0], a[1] - b[1])


def dft4(v):
    a, b = plus(v[0], v[2]), minus(v[0], v[2])
    c, d = plus(v[1], v[3]), minus(v[1], v[3])
    return [plus(a, c), (b[0] - d[1], b[1] + d[0]), minus(a, c), (b[0] + d[1], b[1] - d[0])]


def dft8(v):
    even, odd = dft4(v[0::2]), dft4(v[1::2])
    odd = [turned(odd[t], t, 8) for t in range(4)]
    return [plus(e, o) for e, o in zip(even, odd)] + [minus(e, o) for e, o in zip(even, odd)]


def x_kernel(which, rows_local, *refs):
    n_in = 2 if which == 2 else 3
    ins, (matrix, twist, out, stage, lines, spread) = refs[:n_in], refs[n_in:]
    step = pl.program_id(0)
    scale = 2.0 * math.pi / GRID
    lane = lax.broadcasted_iota(jnp.int32, (16, 128), 1)
    row = lax.broadcasted_iota(jnp.int32, (16, 128), 0)
    start = lax.axis_index(("row", "col")) * rows_local + step * 16
    ky = row + start
    wave_y = jnp.where(ky >= GRID // 2, ky - GRID, ky).astype(jnp.float32) * scale

    def tile(ref, part, q):
        return ref[0, part, :, pl.ds(q * 128, 128)].astype(jnp.float32)

    def wave_x(q):
        base = q * 128 - (GRID if q >= 16 else 0)
        return (lane + base).astype(jnp.float32) * scale

    def curl(q):
        if which == 2:
            u, v = ins
            wx = wave_x(q)
            return (
                wave_y * tile(u, 1, q) - wx * tile(v, 1, q),
                wx * tile(v, 0, q) - wave_y * tile(u, 0, q),
            )
        w, f, g = ins
        step_re = tile(g, 0, q) - tile(f, 0, q)
        step_im = tile(g, 1, q) - tile(f, 1, q)
        if which == 0:
            return (-wave_y * tile(w, 1, q) - step_re, wave_y * tile(w, 0, q) - step_im)
        wx = wave_x(q)
        return (step_re + wx * tile(w, 1, q), step_im - wx * tile(w, 0, q))

    for a in range(8):
        for b, value in enumerate(dft4([curl(a + 8 * t) for t in range(4)])):
            value = turned(value, a * b, 32)
            stage[0, b * 8 + a] = value[0]
            stage[1, b * 8 + a] = value[1]
    for b in range(4):
        for t, value in enumerate(dft8([(stage[0, b * 8 + a], stage[1, b * 8 + a]) for a in range(8)])):
            n = b + 4 * t
            c, s = twist[0, n : n + 1, :], twist[1, n : n + 1, :]
            at = pl.ds(((n % 16) * 2 + n // 16) * 64 + step * 16, 16)
            lines[at, 0:128] = (value[0] * c - value[1] * s).astype(jnp.bfloat16)
            lines[at, 128:256] = (value[0] * s + value[1] * c).astype(jnp.bfloat16)

    @pl.when(step == 3)
    def _():
        for pair in range(8):
            got = lax.dot_general(
                matrix[...], lines[pl.ds(pair * 256, 256), :], NT, preferred_element_type=jnp.float32
            )
            got = got[0:256] + got[256:512]
            for half in range(2):
                n16 = pair * 2 + half
                for s in range(2):
                    for c in range(2):
                        at = (s * 2 + c) * 64
                        spread[pl.ds(c * 32 + s * 16 + n16, 64, stride=64), :] = got[
                            at : at + 64, half * 128 : half * 128 + 128
                        ]
        for b in range(64):
            out[b] = spread[pl.ds(b * 64, 64), :].astype(jnp.bfloat16)


def x_transform(which, fields, x_matrix, x_twist):
    rows_local = fields[0][0].shape[2]
    specs = [
        pl.BlockSpec((1, 2, 16, GRID), lambda i, comp=comp: (comp, 0, i, 0)) for _, comp in fields
    ] + [
        pl.BlockSpec((512, 256), lambda i: (0, 0)),
        pl.BlockSpec((2, 32, 128), lambda i: (0, 0, 0)),
    ]
    return pl.pallas_call(
        lambda *refs: x_kernel(which, rows_local, *refs),
        grid=(rows_local // 16,),
        in_specs=specs,
        out_specs=pl.BlockSpec((64, 64, 128), lambda i: (0, 0, 0)),
        out_shape=jax.ShapeDtypeStruct((64, 64, 128), jnp.bfloat16),
        scratch_shapes=[
            pltpu.VMEM((2, 32, 16, 128), jnp.float32),
            pltpu.VMEM((2048, 256), jnp.bfloat16),
            pltpu.VMEM((4096, 128), jnp.float32),
        ],
        compiler_params=pltpu.CompilerParams(vmem_limit_bytes=VMEM_LIMIT),
        name=f"curl_x_{which}",
    )(*[array for array, _ in fields], x_matrix, x_twist)


def y_lines(source, twist, stage, lines):
    def one(part, carry):
        def load(c, d):
            return source[d, pl.ds(c * 32 + part * 16, 16), :].astype(jnp.float32)

        for a in range(8):
            values = [(load(0, a + 8 * t), load(1, a + 8 * t)) for t in range(8)]
            for b, value in enumerate(dft8(values)):
                value = turned(value, a * b, 64)
                stage[0, b * 8 + a] = value[0]
                stage[1, b * 8 + a] = value[1]
        for b in range(8):
            for t, value in enumerate(dft8([(stage[0, b * 8 + a], stage[1, b * 8 + a]) for a in range(8)])):
                n = b + 8 * t
                c, s = twist[0, n : n + 1, :], twist[1, n : n + 1, :]
                at = pl.ds(n * 32 + part * 16, 16)
                lines[at, 0:128] = (value[0] * c - value[1] * s).astype(jnp.bfloat16)
                lines[at, 128:256] = (value[0] * s + value[1] * c).astype(jnp.bfloat16)
        return carry

    lax.fori_loop(0, 2, one, 0)


def y_kernel(*refs):
    sources, (matrix, twist, out, stage, lines, total) = refs[:3], refs[3:]
    for index, source in enumerate(sources):
        y_lines(source, twist, stage, lines)
        for chunk in range(8):
            got = lax.dot_general(
                matrix[...], lines[pl.ds(chunk * 256, 256), :], NT, preferred_element_type=jnp.float32
            )
            got = got[0:128] + got[128:256]
            at = (slice(None), slice(chunk * 256, chunk * 256 + 256))
            if index == 0:
                total[at] = 1.0 + got * got
            elif index == 1:
                total[at] = total[at] + got * got
            else:
                total[at] = jnp.sqrt(total[at] + got * got)

    def put(h, tile, value):
        value = value.astype(jnp.bfloat16)
        for c in range(4):
            for z in range(2):
                out[z * 4 + c, h * 16 : h * 16 + 16, tile * 128 : tile * 128 + 128] = value[c * 16 : c * 16 + 16]

    for h in range(2):
        rows = slice(h * 64, h * 64 + 64)
        for tile in range(16):
            put(h, tile + 1, total[rows, tile * 128 : tile * 128 + 128])
        put(h, 0, pltpu.roll(total[rows, 15 * 128 : 16 * 128], 1, 0))
        put(h, 17, pltpu.roll(total[rows, 0:128], 63, 0))


def y_transform(sources, y_matrix, y_twist):
    return pl.pallas_call(
        y_kernel,
        out_shape=jax.ShapeDtypeStruct((8, 32, 2304), jnp.bfloat16),
        scratch_shapes=[
            pltpu.VMEM((2, 64, 16, 128), jnp.float32),
            pltpu.VMEM((2048, 256), jnp.bfloat16),
            pltpu.VMEM((128, 2048), jnp.float32),
        ],
        compiler_params=pltpu.CompilerParams(vmem_limit_bytes=VMEM_LIMIT),
        name="y_magnitude",
    )(*sources, y_matrix, y_twist)


def smooth_coefficients():
    w = RELAX
    even = np.polynomial.polynomial.polypow([1 - 6 * w + 2 * w, w], 3)
    odd = np.polynomial.polynomial.polypow([1 - 6 * w - 2 * w, w], 3)
    return (even + odd) / 2, (even - odd) / 2


def smooth_kernel(field, low, high, out, own, other, work, spread):
    own_c, other_c = [[float(v) for v in part] for part in smooth_coefficients()]
    me = lax.axis_index("gz")
    lane = lax.broadcasted_iota(jnp.int32, (16, 128), 1)

    def swapped(a, b, width):
        upper = (lane & width) != 0
        return (
            jnp.where(upper, pltpu.roll(b, width, 1), a),
            jnp.where(upper, b, pltpu.roll(a, 128 - width, 1)),
        )

    def gather(z, target, tile):
        at = pl.ds(pl.multiple_of(tile * 128, 128), 128)
        v = {
            (c, h): field[z * 4 + c, h * 16 : h * 16 + 16, at].astype(jnp.float32)
            for c in range(4)
            for h in range(2)
        }
        edge_low = low[z, :, at].astype(jnp.float32)
        edge_high = high[z, :, at].astype(jnp.float32)
        for ch in range(2):
            p = {}
            for h in range(2):
                p[0, h], p[1, h] = swapped(v[ch * 2, h], v[ch * 2 + 1, h], 64)
            for y1 in range(2):
                s0, s1 = swapped(p[y1, 0], p[y1, 1], 16)
                y00, y01 = swapped(s0, s1, 32)
                target[tile * 4 + y1 * 2, :, ch * 128 : ch * 128 + 128] = y00
                target[tile * 4 + y1 * 2 + 1, :, ch * 128 : ch * 128 + 128] = y01
        for y in range(4):
            right = edge_high if y == 0 else pltpu.roll(edge_high, 128 - 32 * y, 1)
            left = pltpu.roll(edge_low, (96 - 32 * y) % 128, 1) if y != 3 else edge_low
            target[tile * 4 + y, :, 256:384] = jnp.where(lane < 64, right, left)

    def gather_both(tile, carry):
        gather(me, own, tile)
        gather(1 - me, other, tile)
        return carry

    lax.fori_loop(0, 18, gather_both, 0)

    def beside(ref, y, weight=None):
        center = ref[y]
        sides = pltpu.roll(center, 1, 1) + pltpu.roll(center, 383, 1)
        total = sides + (ref[y - 1] + ref[y + 1])
        return total if weight is None else total * weight

    def first(y, carry):
        work[0, y] = own[y] * own_c[2] + other[y] * other_c[2] + beside(own, y, own_c[3])
        return carry

    def second(y, carry):
        work[1, y] = own[y] * own_c[1] + other[y] * other_c[1] + beside(work.at[0], y)
        return carry

    def third(y, carry):
        value = own[y] * own_c[0] + other[y] * other_c[0] + beside(work.at[1], y)
        for half in range(2):
            spread[pl.ds(half * 1024 + y - 4, 16, stride=64), :] = value[:, half * 128 : half * 128 + 128]
        return carry

    lax.fori_loop(2, 70, first, 0)
    lax.fori_loop(3, 69, second, 0)
    lax.fori_loop(4, 68, third, 0)
    for half in range(2):
        out[0, :, half * 128 : half * 128 + 128] = spread[pl.ds(half * 1024, 1024), :]


def smooth(field, low, high):
    return pl.pallas_call(
        smooth_kernel,
        out_shape=jax.ShapeDtypeStruct((1, 1024, 256), jnp.float32),
        scratch_shapes=[
            pltpu.VMEM((72, 16, 384), jnp.float32),
            pltpu.VMEM((72, 16, 384), jnp.float32),
            pltpu.VMEM((2, 72, 16, 384), jnp.float32),
            pltpu.VMEM((2048, 128), jnp.float32),
        ],
        compiler_params=pltpu.CompilerParams(vmem_limit_bytes=VMEM_LIMIT),
        name="smooth",
    )(field, low, high)


def ring(value, axis, steps):
    count = lax.axis_size(axis)
    return lax.ppermute(value, axis, [(i, (i + steps) % count) for i in range(count)])


def shards(velocity_hat):
    x_matrix, x_twist, y_matrix, y_twist = (jnp.asarray(t) for t in tables())
    rows_local = velocity_hat.shape[3]
    parts = velocity_hat.reshape(3, 2, rows_local, GRID)
    next_v = ring(parts[1:2], "gz", 1)
    next_u = ring(parts[0:1], "gz", 1)

    def exchanged(array):
        return lax.all_to_all(array, ("row", "col"), split_axis=0, concat_axis=0, tiled=True)

    line_2 = exchanged(x_transform(2, [(parts, 0), (parts, 1)], x_matrix, x_twist))
    line_0 = exchanged(x_transform(0, [(parts, 2), (parts, 1), (next_v, 0)], x_matrix, x_twist))
    line_1 = exchanged(x_transform(1, [(parts, 2), (parts, 0), (next_u, 0)], x_matrix, x_twist))
    magnitude = y_transform([line_2, line_0, line_1], y_matrix, y_twist)
    field = lax.all_to_all(magnitude, ("gz", "col"), split_axis=0, concat_axis=0, tiled=True)
    by_source = field.reshape(2, 4, 32, 2304)
    high = ring(by_source[:, 0, 0:16], "row", -1)
    low = ring(by_source[:, 3, 16:32], "row", 1)
    return smooth(field, low, high)


def solution(mesh):
    return jax.shard_map(
        shards,
        mesh=mesh,
        in_specs=(P(None, None, "gz", ("row", "col"), None),),
        out_specs=P("gz", "col", "row"),
        check_vma=False,
    )
```

time: 682 us -> 167 us (0.24); the launches traced: 672 us -> 167 us
  local copies, waits for them, and re-layouts: 172 us -> 6.21 us
  matrix products: 157 us -> 0 us
  waiting for transfers between devices: 176 us -> 45.3 us
  other arithmetic: 64.9 us -> 0 us
  Pallas kernels: 0 us -> 41.9 us
  blocking collectives: 66.5 us -> 49.8 us
  starting transfers between devices: 35 us -> 23.6 us
    dot_general x14 -> x0, matrix products: 157 us -> none  [the longest x2 29 us: inverse_transform(): contract(spec_two, turned_real, cos_inner)]
    ppermute x19 -> x4, waiting for transfers between devices: 176 us -> 41.6 us  [ring(): lax.ppermute(value, axis, [(i, (i + steps) % count) for i in range(count)])]
    another operation x8 -> x0, local copies, waits for them, and re-layouts: 58 us -> none  [the longest x4 35.3 us: shards(): spectral_x = jnp.stack([line_real, line_imag], axis=1)]
    pallas_call x0 -> x5, Pallas kernels: none -> 41.9 us  [the longest x1 23 us: smooth(): pl.pallas_call(smooth_kernel, out_shape=jax.ShapeDtypeStruct((1, 1024, 25...]
    unnamed x2 -> x0, other arithmetic: 41.7 us -> none
    ppermute x19 -> x4, starting transfers between devices: 35 us -> 2.57 us  [ring(): lax.ppermute(value, axis, [(i, (i + steps) % count) for i in range(count)])]
    unnamed x15 -> x16, local copies, waits for them, and re-layouts: 31.2 us -> 2.92 us
    squeeze x10 -> x1, local copies, waits for them, and re-layouts: 25.4 us -> 0.02 us  [shards(): high = ring(by_source[:, 0, 0:16], 'row', -1)]
  transfers between devices with their start and end apart: 19 -> 6, of which waited for: 15 -> 6; matrix products, arithmetic and copies ran while one was open for 4% -> 0% of each run, Pallas kernels for 0% -> 8%
where the time goes in v1:
time: 167 us
  blocking collectives  49.8 us (30%)
  waiting for transfers between devices  45.3 us (27%)
  Pallas kernels  41.9 us (25%)
  starting transfers between devices  23.6 us (14%)
  local copies, waits for them, and re-layouts  6.21 us (4%)
    ppermute x4, waiting for transfers between devices, ring(): lax.ppermute(value, axis, [(i, (i + steps) % count) for i in range(count)])  41.6 us
    all_to_all x1, blocking collectives, exchanged(): lax.all_to_all(array, ('row', 'col'), split_axis=0, concat_axis=0, tiled=...  29.9 us
    pallas_call x1, Pallas kernels, smooth(): pl.pallas_call(smooth_kernel, out_shape=jax.ShapeDtypeStruct((1, 1024, 25...  23 us
    all_to_all x2, starting transfers between devices, exchanged(): lax.all_to_all(array, ('row', 'col'), split_axis=0, concat_axis=0, tiled=...  21 us
    all_to_all x1, blocking collectives, shards(): lax.all_to_all(magnitude, ('gz', 'col'), split_axis=0, concat_axis=0, til...  19.8 us
    pallas_call x3, Pallas kernels, x_transform(): pl.pallas_call(lambda *refs: x_kernel(which, rows_local, *refs), grid=(ro...  12.8 us
    pallas_call x1, Pallas kernels, y_transform(): pl.pallas_call(y_kernel, out_shape=jax.ShapeDtypeStruct((8, 32, 2304), jn...  6.11 us
    all_to_all x2, waiting for transfers between devices, exchanged(): lax.all_to_all(array, ('row', 'col'), split_axis=0, concat_axis=0, tiled=...  3.7 us
  transfers between devices with their start and end apart: 6, of which 6 were waited for; matrix products, arithmetic and copies ran while one was open for 0% of the time, Pallas kernels for 8%

profile of v1, /device:TPU:0, one launch (start us, length us, event | category | flops | bytes accessed | tf_op | source)
XLA Modules:
  0.0 166.9 jit_solution(15865374558308285731)
XLA Ops:
  0.0 0.0 copy-start
  0.0 3.3 %slice_bitcast_fusion = (bf16[1,2,64,4096]{3,2,1,0:T(8,128)(2,1)}, bf16[1,2,64,4096]{3,2,1,0:T(8,128)(2,1)}) fusion(bf16[3,2,1,64,4096]{4,3,1,2,0:T(8,128)(2,1)} %bitcast.15), kind=kLoop, calls=%fused_computation | loop fusion | bytes 4194304 | tf_op jit(solution)/shard_map/slice | solution.py:349
  3.3 1.7 collective-permute-start.1
  4.9 0.0 copy-done
  4.9 0.0 copy-done.4
  4.9 0.0 copy-done.5
  4.9 3.2 %curl_x_2.1 = bf16[64,64,128]{2,1,0:T(8,128)(2,1)S(1)} custom-call(bf16[3,2,64,4096]{3,2,1,0:T(8,128)(2,1)S(1)} %bitcast.16, bf16[3,2,64,4096]{3,2,1,0:T(8,128)(2,1)S(1)} %bitcast.17, bf16[512,256]{1,0:T(8,128)(2,1)S(1)} %copy-done.4, f32[2,32,128]{2,1,0:T(8,128)S(1)} %copy-done.5), custom_call_target="tpu_custom_call" | custom-call | tf_op jit(solution)/shard_map/curl_x_2/pallas_call | solution.py:164
  8.2 0.0 copy-start.3
  8.2 1.0 copy-done.3
  9.2 11.4 %all-to-all-start = ((bf16[64,64,128]{2,1,0:T(8,128)(2,1)}), bf16[64,64,128]{2,1,0:T(8,128)(2,1)}, u32[]{:S(2)}, u32[]{:S(2)}) async-start(bf16[64,64,128]{2,1,0:T(8,128)(2,1)} %copy-done.3), calls=%async_computation | async-start | bytes 2097152 | tf_op jit(solution)/shard_map/all_to_all | solution.py:352
  20.6 0.2 collective-permute-start
  20.8 17.3 %collective-permute-done.1.refs_2_ = bf16[1,2,64,4096]{3,2,1,0:T(8,128)(2,1)} collective-permute-done((bf16[1,2,64,4096]{3,2,1,0:T(8,128)(2,1)}, bf16[1,2,64,4096]{3,2,1,0:T(8,128)(2,1)}, u32[]{:S(2)}, u32[]{:S(2)}) %collective-permute-start.1) | collective-permute-done | bytes 1048608 | tf_op jit(solution)/shard_map/ppermute | solution.py:341
  38.1 4.8 %curl_x_1.1 = bf16[64,64,128]{2,1,0:T(8,128)(2,1)S(1)} custom-call(bf16[3,2,64,4096]{3,2,1,0:T(8,128)(2,1)S(1)} %bitcast.18, bf16[3,2,64,4096]{3,2,1,0:T(8,128)(2,1)S(1)} %bitcast.19, bf16[1,2,64,4096]{3,2,1,0:T(8,128)(2,1)} %collective-permute-done.1.refs_2_, bf16[512,256]{1,0:T(8,128)(2,1)S(1)} %copy-done.4, f32[2,32,128]{2,1,0:T(8,128)S(1)} %copy-done.5), custom_call_target="tpu_custom_call" | custom-call | tf_op jit(solution)/shard_map/curl_x_1/pallas_call | solution.py:164
  42.9 0.0 copy-start.1
  42.9 1.0 copy-done.1
  43.9 2.1 %all-to-all-done.refs_0_ = bf16[64,64,128]{2,1,0:T(8,128)(2,1)} async-done(((bf16[64,64,128]{2,1,0:T(8,128)(2,1)}), bf16[64,64,128]{2,1,0:T(8,128)(2,1)}, u32[]{:S(2)}, u32[]{:S(2)}) %all-to-all-start) | async-done | bytes 1048608 | tf_op jit(solution)/shard_map/all_to_all | solution.py:352
  46.0 9.6 %all-to-all-start.2 = ((bf16[64,64,128]{2,1,0:T(8,128)(2,1)}), bf16[64,64,128]{2,1,0:T(8,128)(2,1)}, u32[]{:S(2)}, u32[]{:S(2)}) async-start(bf16[64,64,128]{2,1,0:T(8,128)(2,1)} %copy-done.1), calls=%async_computation.2 | async-start | bytes 2097152 | tf_op jit(solution)/shard_map/all_to_all | solution.py:352
  55.6 16.1 %collective-permute-done.refs_2_ = bf16[1,2,64,4096]{3,2,1,0:T(8,128)(2,1)} collective-permute-done((bf16[1,2,64,4096]{3,2,1,0:T(8,128)(2,1)}, bf16[1,2,64,4096]{3,2,1,0:T(8,128)(2,1)}, u32[]{:S(2)}, u32[]{:S(2)}) %collective-permute-start) | collective-permute-done | bytes 1048608 | tf_op jit(solution)/shard_map/ppermute | solution.py:341
  71.8 4.8 %curl_x_0.1 = bf16[64,64,128]{2,1,0:T(8,128)(2,1)S(1)} custom-call(bf16[3,2,64,4096]{3,2,1,0:T(8,128)(2,1)S(1)} %bitcast.20, bf16[3,2,64,4096]{3,2,1,0:T(8,128)(2,1)S(1)} %bitcast.21, bf16[1,2,64,4096]{3,2,1,0:T(8,128)(2,1)} %collective-permute-done.refs_2_, bf16[512,256]{1,0:T(8,128)(2,1)S(1)} %copy-done.4, f32[2,32,128]{2,1,0:T(8,128)S(1)} %copy-done.5), custom_call_target="tpu_custom_call" | custom-call | tf_op jit(solution)/shard_map/curl_x_0/pallas_call | solution.py:164
  76.5 0.0 copy-start.2
  76.6 1.0 copy-done.2
  77.5 1.6 all-to-all-done.2.refs_2_
  79.1 29.9 %all_to_all.20.refs_1_ = bf16[64,64,128]{2,1,0:T(8,128)(2,1)S(1)} all-to-all(bf16[64,64,128]{2,1,0:T(8,128)(2,1)} %copy-done.2), channel_id=1, replica_groups=mesh['row'=16,'col'=4,'gz'=2] {'row','col'}, dimensions={0} | all-to-all | bytes 2097152 | tf_op jit(solution)/shard_map/all_to_all | solution.py:352
  109.0 0.0 copy-done.6
  109.0 0.0 copy-done.7
  109.0 6.1 %y_magnitude.1 = bf16[8,32,2304]{2,1,0:T(8,128)(2,1)S(1)} custom-call(bf16[64,64,128]{2,1,0:T(8,128)(2,1)} %all-to-all-done.refs_0_, bf16[64,64,128]{2,1,0:T(8,128)(2,1)S(1)} %all_to_all.20.refs_1_, bf16[64,64,128]{2,1,0:T(8,128)(2,1)} %all-to-all-done.2.refs_2_, bf16[256,256]{1,0:T(8,128)(2,1)S(1)} %copy-done.6, f32[2,64,128]{2,1,0:T(8,128)S(1)} %copy-done.7), custom_call_target="tpu_custom_call" | custom-call | tf_op jit(solution)/shard_map/y_magnitude/pallas_call | solution.py:235
  115.2 19.8 %all_to_all.21.field = bf16[8,32,2304]{2,1,0:T(8,128)(2,1)S(1)} all-to-all(bf16[8,32,2304]{2,1,0:T(8,128)(2,1)S(1)} %y_magnitude.1), channel_id=1, replica_groups=mesh['row'=16,'col'=4,'gz'=2] {'gz','col'}, dimensions={0} | all-to-all | bytes 2359296 | tf_op jit(solution)/shard_map/all_to_all | solution.py:358
  135.0 0.7 collective-permute-start.3
  135.7 0.0 collective-permute-start.2
  135.7 2.7 %collective-permute-done.3.high = bf16[2,16,2304]{2,1,0:T(8,128)(2,1)S(1)} collective-permute-done((bf16[2,16,2304]{2,1,0:T(8,128)(2,1)S(1)}, bf16[2,16,2304]{2,1,0:T(8,128)(2,1)S(1)}, u32[]{:S(2)}, u32[]{:S(2)}) %collective-permute-start.3) | collective-permute-done | bytes 147488 | tf_op jit(solution)/shard_map/ppermute | solution.py:341
  138.4 5.5 %collective-permute-done.2.low = bf16[2,16,2304]{2,1,0:T(8,128)(2,1)S(1)} collective-permute-done((bf16[2,16,2304]{2,1,0:T(8,128)(2,1)S(1)}, bf16[2,16,2304]{2,1,0:T(8,128)(2,1)S(1)}, u32[]{:S(2)}, u32[]{:S(2)}) %collective-permute-start.2) | collective-permute-done | bytes 147488 | tf_op jit(solution)/shard_map/ppermute | solution.py:341
  143.9 23.0 %smooth.1 = f32[1,1024,256]{2,1,0:T(8,128)} custom-call(bf16[8,32,2304]{2,1,0:T(8,128)(2,1)S(1)} %all_to_all.21.field, bf16[2,16,2304]{2,1,0:T(8,128)(2,1)S(1)} %collective-permute-done.2.low, bf16[2,16,2304]{2,1,0:T(8,128)(2,1)S(1)} %collective-permute-done.3.high), custom_call_target="tpu_custom_call" | custom-call | tf_op jit(solution)/shard_map/smooth/pallas_call | solution.py:325
  (5 shorter events, 0.0 us)
Async XLA Ops:
  0.0 4.9 %copy-start = (bf16[3,2,1,64,4096]{4,3,2,1,0:T(8,128)(2,1)S(1)}, bf16[3,2,1,64,4096]{4,3,2,1,0:T(8,128)(2,1)}, u32[]{:S(2)}) copy-start(bf16[3,2,1,64,4096]{4,3,2,1,0:T(8,128)(2,1)} %param.5) | copy-start | bytes 9437188
  0.0 4.9 %copy-start.4 = (bf16[512,256]{1,0:T(8,128)(2,1)S(1)}, bf16[512,256]{1,0:T(8,128)(2,1)}, u32[]{:S(2)}) copy-start(bf16[512,256]{1,0:T(8,128)(2,1)} %constant.8.clone.refs_2_.refs_3_) | copy-start | bytes 786436
  0.0 4.9 %copy-start.5 = (f32[2,32,128]{2,1,0:T(8,128)S(1)}, f32[2,32,128]{2,1,0:T(8,128)}, u32[]{:S(2)}) copy-start(f32[2,32,128]{2,1,0:T(8,128)} %constant.9.clone.refs_3_.refs_4_) | copy-start | bytes 98308
  3.3 34.8 %collective-permute-start.1 = (bf16[1,2,64,4096]{3,2,1,0:T(8,128)(2,1)}, bf16[1,2,64,4096]{3,2,1,0:T(8,128)(2,1)}, u32[]{:S(2)}, u32[]{:S(2)}) collective-permute-start(bf16[1,2,64,4096]{3,2,1,0:T(8,128)(2,1)} %get-tuple-element.5), channel_id=1, source_target_pairs={{0,1},{1,0},{2,3},{3,2},{4,5},{5,4},{6,7},{7,6},{8,9},{9,8},{10,11... | collective-permute-start | bytes 3145736 | tf_op jit(solution)/shard_map/ppermute | solution.py:341
  8.2 1.0 copy-start.3
  9.2 36.9 %all-to-all-start = ((bf16[64,64,128]{2,1,0:T(8,128)(2,1)}), bf16[64,64,128]{2,1,0:T(8,128)(2,1)}, u32[]{:S(2)}, u32[]{:S(2)}) async-start(bf16[64,64,128]{2,1,0:T(8,128)(2,1)} %copy-done.3), calls=%async_computation | async-start | bytes 2097152 | tf_op jit(solution)/shard_map/all_to_all | solution.py:352
  20.6 51.2 %collective-permute-start = (bf16[1,2,64,4096]{3,2,1,0:T(8,128)(2,1)}, bf16[1,2,64,4096]{3,2,1,0:T(8,128)(2,1)}, u32[]{:S(2)}, u32[]{:S(2)}) collective-permute-start(bf16[1,2,64,4096]{3,2,1,0:T(8,128)(2,1)} %get-tuple-element.6), channel_id=1, source_target_pairs={{0,1},{1,0},{2,3},{3,2},{4,5},{5,4},{6,7},{7,6},{8,9},{9,8},{10,11... | collective-permute-start | bytes 3145736 | tf_op jit(solution)/shard_map/ppermute | solution.py:341
  42.9 1.0 copy-start.1
  46.0 33.1 %all-to-all-start.2 = ((bf16[64,64,128]{2,1,0:T(8,128)(2,1)}), bf16[64,64,128]{2,1,0:T(8,128)(2,1)}, u32[]{:S(2)}, u32[]{:S(2)}) async-start(bf16[64,64,128]{2,1,0:T(8,128)(2,1)} %copy-done.1), calls=%async_computation.2 | async-start | bytes 2097152 | tf_op jit(solution)/shard_map/all_to_all | solution.py:352
  76.5 1.0 copy-start.2
  77.5 31.5 %copy-start.6 = (bf16[256,256]{1,0:T(8,128)(2,1)S(1)}, bf16[256,256]{1,0:T(8,128)(2,1)}, u32[]{:S(2)}) copy-start(bf16[256,256]{1,0:T(8,128)(2,1)} %constant.10.clone.refs_3_) | copy-start | bytes 393220
  77.5 31.5 %copy-start.7 = (f32[2,64,128]{2,1,0:T(8,128)S(1)}, f32[2,64,128]{2,1,0:T(8,128)}, u32[]{:S(2)}) copy-start(f32[2,64,128]{2,1,0:T(8,128)} %constant.11.clone.refs_4_) | copy-start | bytes 196612
  135.0 3.4 %collective-permute-start.3 = (bf16[2,16,2304]{2,1,0:T(8,128)(2,1)S(1)}, bf16[2,16,2304]{2,1,0:T(8,128)(2,1)S(1)}, u32[]{:S(2)}, u32[]{:S(2)}) collective-permute-start(bf16[2,16,2304]{2,1,0:T(8,128)(2,1)S(1)} %get-tuple-element.7), channel_id=1, source_target_pairs={{0,120},{8,0},{16,8},{24,16},{32,24},{40,32},{48,40},{56,48},{64,5... | collective-permute-start | bytes 442376 | tf_op jit(solution)/shard_map/ppermute | solution.py:341
  135.7 8.2 %collective-permute-start.2 = (bf16[2,16,2304]{2,1,0:T(8,128)(2,1)S(1)}, bf16[2,16,2304]{2,1,0:T(8,128)(2,1)S(1)}, u32[]{:S(2)}, u32[]{:S(2)}) collective-permute-start(bf16[2,16,2304]{2,1,0:T(8,128)(2,1)S(1)} %get-tuple-element.8), channel_id=1, source_target_pairs={{0,8},{8,16},{16,24},{24,32},{32,40},{40,48},{48,56},{56,64},{64,7... | collective-permute-start | bytes 442376 | tf_op jit(solution)/shard_map/ppermute | solution.py:341

commit v2 on v1

--- a/solution.py
+++ b/solution.py
@@ -200,22 +200,35 @@
     lax.fori_loop(0, 2, one, 0)
 
 
-def y_kernel(*refs):
-    sources, (matrix, twist, out, stage, lines, total) = refs[:3], refs[3:]
-    for index, source in enumerate(sources):
-        y_lines(source, twist, stage, lines)
-        for chunk in range(8):
-            got = lax.dot_general(
-                matrix[...], lines[pl.ds(chunk * 256, 256), :], NT, preferred_element_type=jnp.float32
-            )
-            got = got[0:128] + got[128:256]
-            at = (slice(None), slice(chunk * 256, chunk * 256 + 256))
-            if index == 0:
-                total[at] = 1.0 + got * got
-            elif index == 1:
-                total[at] = total[at] + got * got
-            else:
-                total[at] = jnp.sqrt(total[at] + got * got)
+def y_squares(source, matrix, twist, stage, lines, add):
+    y_lines(source, twist, stage, lines)
+    for chunk in range(8):
+        got = lax.dot_general(
+            matrix[...], lines[pl.ds(chunk * 256, 256), :], NT, preferred_element_type=jnp.float32
+        )
+        got = got[0:128] + got[128:256]
+        add((slice(None), slice(chunk * 256, chunk * 256 + 256)), got * got)
+
+
+def y_first(source, matrix, twist, out, stage, lines):
+    def add(at, square):
+        out[at] = 1.0 + square
+
+    y_squares(source, matrix, twist, stage, lines, add)
+
+
+def y_next(source, before, matrix, twist, out, stage, lines):
+    def add(at, square):
+        out[at] = before[at] + square
+
+    y_squares(source, matrix, twist, stage, lines, add)
+
+
+def y_last(source, before, matrix, twist, out, stage, lines, total):
+    def add(at, square):
+        total[at] = jnp.sqrt(before[at] + square)
+
+    y_squares(source, matrix, twist, stage, lines, add)
 
     def put(h, tile, value):
         value = value.astype(jnp.bfloat16)
@@ -231,18 +244,18 @@
         put(h, 17, pltpu.roll(total[rows, 0:128], 63, 0))
 
 
-def y_transform(sources, y_matrix, y_twist):
+def y_transform(kernel, source, before, y_matrix, y_twist):
+    last = kernel is y_last
+    sums = jax.ShapeDtypeStruct((128, 2048), jnp.float32)
+    scratch = [pltpu.VMEM((2, 64, 16, 128), jnp.float32), pltpu.VMEM((2048, 256), jnp.bfloat16)]
     return pl.pallas_call(
-        y_kernel,
-        out_shape=jax.ShapeDtypeStruct((8, 32, 2304), jnp.bfloat16),
-        scratch_shapes=[
-            pltpu.VMEM((2, 64, 16, 128), jnp.float32),
-            pltpu.VMEM((2048, 256), jnp.bfloat16),
-            pltpu.VMEM((128, 2048), jnp.float32),
-        ],
+        kernel,
+        out_shape=jax.ShapeDtypeStruct((8, 32, 2304), jnp.bfloat16) if last else sums,
+        scratch_shapes=scratch + ([pltpu.VMEM((128, 2048), jnp.float32)] if last else []),
         compiler_params=pltpu.CompilerParams(vmem_limit_bytes=VMEM_LIMIT),
-        name="y_magnitude",
-    )(*sources, y_matrix, y_twist)
+        cost_estimate=pl.CostEstimate(flops=2**28, bytes_accessed=2**22, transcendentals=0),
+        name=kernel.__name__,
+    )(source, *before, y_matrix, y_twist)
 
 
 def smooth_coefficients():
@@ -252,8 +265,7 @@
     return (even + odd) / 2, (even - odd) / 2
 
 
-def smooth_kernel(field, low, high, out, own, other, work, spread):
-    own_c, other_c = [[float(v) for v in part] for part in smooth_coefficients()]
+def regroup_kernel(field, own, other):
     me = lax.axis_index("gz")
     lane = lax.broadcasted_iota(jnp.int32, (16, 128), 1)
 
@@ -264,76 +276,140 @@
             jnp.where(upper, b, pltpu.roll(a, 128 - width, 1)),
         )
 
-    def gather(z, target, tile):
+    def regroup(z, target, tile):
         at = pl.ds(pl.multiple_of(tile * 128, 128), 128)
-        v = {
-            (c, h): field[z * 4 + c, h * 16 : h * 16 + 16, at].astype(jnp.float32)
-            for c in range(4)
-            for h in range(2)
-        }
-        edge_low = low[z, :, at].astype(jnp.float32)
-        edge_high = high[z, :, at].astype(jnp.float32)
         for ch in range(2):
+            v = {
+                (c, h): field[z * 4 + ch * 2 + c, h * 16 : h * 16 + 16, at].astype(jnp.float32)
+                for c in range(2)
+                for h in range(2)
+            }
             p = {}
             for h in range(2):
-                p[0, h], p[1, h] = swapped(v[ch * 2, h], v[ch * 2 + 1, h], 64)
+                p[0, h], p[1, h] = swapped(v[0, h], v[1, h], 64)
             for y1 in range(2):
                 s0, s1 = swapped(p[y1, 0], p[y1, 1], 16)
                 y00, y01 = swapped(s0, s1, 32)
                 target[tile * 4 + y1 * 2, :, ch * 128 : ch * 128 + 128] = y00
                 target[tile * 4 + y1 * 2 + 1, :, ch * 128 : ch * 128 + 128] = y01
-        for y in range(4):
-            right = edge_high if y == 0 else pltpu.roll(edge_high, 128 - 32 * y, 1)
-            left = pltpu.roll(edge_low, (96 - 32 * y) % 128, 1) if y != 3 else edge_low
-            target[tile * 4 + y, :, 256:384] = jnp.where(lane < 64, right, left)
-
-    def gather_both(tile, carry):
-        gather(me, own, tile)
-        gather(1 - me, other, tile)
+
+    def both(step, carry):
+        for t in range(3):
+            regroup(me, own, step * 3 + t)
+            regroup(1 - me, other, step * 3 + t)
         return carry
 
-    lax.fori_loop(0, 18, gather_both, 0)
-
-    def beside(ref, y, weight=None):
-        center = ref[y]
+    lax.fori_loop(0, 6, both, 0)
+
+
+def regroup(field):
+    return pl.pallas_call(
+        regroup_kernel,
+        out_shape=[jax.ShapeDtypeStruct((72, 16, 256), jnp.float32)] * 2,
+        compiler_params=pltpu.CompilerParams(vmem_limit_bytes=VMEM_LIMIT),
+        cost_estimate=pl.CostEstimate(flops=2**24, bytes_accessed=2**23, transcendentals=0),
+        name="regroup",
+    )(field)
+
+
+def smooth_kernel(own, other, low, high, out, own_edge, other_edge, work, spread):
+    own_c, other_c = [[float(v) for v in part] for part in smooth_coefficients()]
+    me = lax.axis_index("gz")
+    lane = lax.broadcasted_iota(jnp.int32, (16, 128), 1)
+
+    def edges(step, carry):
+        for t in range(3):
+            tile = step * 3 + t
+            at = pl.ds(pl.multiple_of(tile * 128, 128), 128)
+            for z, target in ((me, own_edge), (1 - me, other_edge)):
+                left = low[z, :, at].astype(jnp.float32)
+                right = high[z, :, at].astype(jnp.float32)
+                for y in range(4):
+                    target[tile * 4 + y] = jnp.where(
+                        lane < 64,
+                        pltpu.roll(right, 128 - 32 * y, 1) if y else right,
+                        pltpu.roll(left, 96 - 32 * y, 1) if y < 3 else left,
+                    )
+        return carry
+
+    lax.fori_loop(0, 6, edges, 0)
+
+    def beside(ref, y, center):
         sides = pltpu.roll(center, 1, 1) + pltpu.roll(center, 383, 1)
-        total = sides + (ref[y - 1] + ref[y + 1])
-        return total if weight is None else total * weight
-
-    def first(y, carry):
-        work[0, y] = own[y] * own_c[2] + other[y] * other_c[2] + beside(own, y, own_c[3])
-        return carry
-
-    def second(y, carry):
-        work[1, y] = own[y] * own_c[1] + other[y] * other_c[1] + beside(work.at[0], y)
-        return carry
-
-    def third(y, carry):
-        value = own[y] * own_c[0] + other[y] * other_c[0] + beside(work.at[1], y)
+        return sides + (ref(y - 1) + ref(y + 1))
+
+    def own_at(y):
+        return jnp.concatenate([own[y], own_edge[y]], axis=1)
+
+    def other_at(y):
+        return jnp.concatenate([other[y], other_edge[y]], axis=1)
+
+    def each(begin, end, unroll, body):
+        def some(step, carry):
+            for t in range(unroll):
+                body(begin + step * unroll + t)
+            return carry
+
+        lax.fori_loop(0, (end - begin) // unroll, some, 0)
+
+    def first(y):
+        center = own_at(y)
+        work[0, y] = center * own_c[2] + other_at(y) * other_c[2] + beside(own_at, y, center) * own_c[3]
+
+    def second(y):
+        center = work[0, y]
+        work[1, y] = own_at(y) * own_c[1] + other_at(y) * other_c[1] + beside(lambda i: work[0, i], y, center)
+
+    def third(y):
+        center = work[1, y]
+        value = beside(lambda i: work[1, i], y, center)[:, 0:256]
+        value = own[y] * own_c[0] + other[y] * other_c[0] + value
         for half in range(2):
             spread[pl.ds(half * 1024 + y - 4, 16, stride=64), :] = value[:, half * 128 : half * 128 + 128]
-        return carry
-
-    lax.fori_loop(2, 70, first, 0)
-    lax.fori_loop(3, 69, second, 0)
-    lax.fori_loop(4, 68, third, 0)
+
+    each(2, 70, 4, first)
+    each(3, 69, 6, second)
+    each(4, 68, 4, third)
     for half in range(2):
         out[0, :, half * 128 : half * 128 + 128] = spread[pl.ds(half * 1024, 1024), :]
 
 
-def smooth(field, low, high):
+def smooth(own, other, low, high):
     return pl.pallas_call(
         smooth_kernel,
         out_shape=jax.ShapeDtypeStruct((1, 1024, 256), jnp.float32),
         scratch_shapes=[
-            pltpu.VMEM((72, 16, 384), jnp.float32),
-            pltpu.VMEM((72, 16, 384), jnp.float32),
+            pltpu.VMEM((72, 16, 128), jnp.float32),
+            pltpu.VMEM((72, 16, 128), jnp.float32),
             pltpu.VMEM((2, 72, 16, 384), jnp.float32),
             pltpu.VMEM((2048, 128), jnp.float32),
         ],
         compiler_params=pltpu.CompilerParams(vmem_limit_bytes=VMEM_LIMIT),
         name="smooth",
-    )(field, low, high)
+    )(own, other, low, high)
+
+
+def copy_kernel(parts, u, v, sems):
+    copies = [
+        pltpu.make_async_copy(parts.at[pl.ds(i, 1)], target, sems.at[i]) for i, target in enumerate((u, v))
+    ]
+    for copy in copies:
+        copy.start()
+    for copy in copies:
+        copy.wait()
+
+
+def copy_uv(parts):
+    shape = jax.ShapeDtypeStruct((1,) + parts.shape[1:], parts.dtype)
+    return pl.pallas_call(
+        copy_kernel,
+        in_specs=[pl.BlockSpec(memory_space=pl.ANY)],
+        out_specs=[pl.BlockSpec(memory_space=pltpu.VMEM)] * 2,
+        out_shape=[shape, shape],
+        scratch_shapes=[pltpu.SemaphoreType.DMA((2,))],
+        compiler_params=pltpu.CompilerParams(vmem_limit_bytes=VMEM_LIMIT),
+        name="copy_uv",
+    )(parts)
 
 
 def ring(value, axis, steps):
@@ -345,21 +421,25 @@
     x_matrix, x_twist, y_matrix, y_twist = (jnp.asarray(t) for t in tables())
     rows_local = velocity_hat.shape[3]
     parts = velocity_hat.reshape(3, 2, rows_local, GRID)
-    next_v = ring(parts[1:2], "gz", 1)
-    next_u = ring(parts[0:1], "gz", 1)
+    u, v = copy_uv(parts)
+    next_u = ring(u, "gz", 1)
+    next_v = ring(v, "gz", 1)
 
     def exchanged(array):
         return lax.all_to_all(array, ("row", "col"), split_axis=0, concat_axis=0, tiled=True)
 
     line_2 = exchanged(x_transform(2, [(parts, 0), (parts, 1)], x_matrix, x_twist))
+    line_1 = exchanged(x_transform(1, [(parts, 2), (parts, 0), (next_u, 0)], x_matrix, x_twist))
     line_0 = exchanged(x_transform(0, [(parts, 2), (parts, 1), (next_v, 0)], x_matrix, x_twist))
-    line_1 = exchanged(x_transform(1, [(parts, 2), (parts, 0), (next_u, 0)], x_matrix, x_twist))
-    magnitude = y_transform([line_2, line_0, line_1], y_matrix, y_twist)
+    squares = y_transform(y_first, line_2, (), y_matrix, y_twist)
+    squares = y_transform(y_next, line_1, (squares,), y_matrix, y_twist)
+    magnitude = y_transform(y_last, line_0, (squares,), y_matrix, y_twist)
     field = lax.all_to_all(magnitude, ("gz", "col"), split_axis=0, concat_axis=0, tiled=True)
     by_source = field.reshape(2, 4, 32, 2304)
     high = ring(by_source[:, 0, 0:16], "row", -1)
     low = ring(by_source[:, 3, 16:32], "row", 1)
-    return smooth(field, low, high)
+    own, other = regroup(field)
+    return smooth(own, other, low, high)
 
 
 def solution(mesh):

time: 167 us -> 149 us (0.89)
  blocking collectives: 49.8 us -> 19.8 us
  waiting for transfers between devices: 45.3 us -> 57.4 us
  Pallas kernels: 41.9 us -> 31.1 us
  starting transfers between devices: 23.6 us -> 33.8 us
    all_to_all x1 -> x0, blocking collectives: 29.9 us -> none  [exchanged(): lax.all_to_all(array, ('row', 'col'), split_axis=0, concat_axis=0, tiled=...]
    pallas_call x1, Pallas kernels: 23 us -> 7.87 us  [smooth(): pl.pallas_call(smooth_kernel, out_shape=jax.ShapeDtypeStruct((1, 1024, 25...]
    all_to_all x2 -> x3, waiting for transfers between devices: 3.7 us -> 17.7 us  [exchanged(): lax.all_to_all(array, ('row', 'col'), split_axis=0, concat_axis=0, tiled=...]
    all_to_all x2 -> x3, starting transfers between devices: 21 us -> 31.3 us  [exchanged(): lax.all_to_all(array, ('row', 'col'), split_axis=0, concat_axis=0, tiled=...]
    pallas_call x1 -> x5, Pallas kernels: 6.11 us -> 10.4 us  [the longest x3 7.35 us: y_transform(): pl.pallas_call(kernel, out_shape=jax.ShapeDtypeStruct((8, 32, 2304), jnp....]
    slice x1 -> x0, local copies, waits for them, and re-layouts: 3.27 us -> none  [shards(): next_u = ring(parts[0:1], 'gz', 1)]
    unnamed x16 -> x20, local copies, waits for them, and re-layouts: 2.92 us -> 5.78 us
    ppermute x4, waiting for transfers between devices: 41.6 us -> 39.6 us  [ring(): lax.ppermute(value, axis, [(i, (i + steps) % count) for i in range(count)])]
  transfers between devices with their start and end apart: 6 -> 7, of which waited for: 6 -> 7; matrix products, arithmetic and copies ran while one was open for 0% -> 0% of each run, Pallas kernels for 8% -> 14%
where the time goes in v2:
time: 149 us; the launch traced here: 148 us
  waiting for transfers between devices  57.4 us (39%)
  starting transfers between devices  33.8 us (23%)
  Pallas kernels  31.1 us (21%)
  blocking collectives  19.8 us (13%)
  local copies, waits for them, and re-layouts  5.8 us (4%)
    ppermute x4, waiting for transfers between devices, ring(): lax.ppermute(value, axis, [(i, (i + steps) % count) for i in range(count)])  39.6 us
    all_to_all x3, starting transfers between devices, exchanged(): lax.all_to_all(array, ('row', 'col'), split_axis=0, concat_axis=0, tiled=...  31.3 us
    all_to_all x1, blocking collectives, shards(): lax.all_to_all(magnitude, ('gz', 'col'), split_axis=0, concat_axis=0, til...  19.8 us
    all_to_all x3, waiting for transfers between devices, exchanged(): lax.all_to_all(array, ('row', 'col'), split_axis=0, concat_axis=0, tiled=...  17.7 us
    pallas_call x3, Pallas kernels, x_transform(): pl.pallas_call(lambda *refs: x_kernel(which, rows_local, *refs), grid=(ro...  12.8 us
    pallas_call x1, Pallas kernels, smooth(): pl.pallas_call(smooth_kernel, out_shape=jax.ShapeDtypeStruct((1, 1024, 25...  7.87 us
    pallas_call x3, Pallas kernels, y_transform(): pl.pallas_call(kernel, out_shape=jax.ShapeDtypeStruct((8, 32, 2304), jnp....  7.35 us
    unnamed x20, local copies, waits for them, and re-layouts  5.78 us
  transfers between devices with their start and end apart: 7, of which 7 were waited for; matrix products, arithmetic and copies ran while one was open for 0% of the time, Pallas kernels for 14%

profile of v2, /device:TPU:0, one launch (start us, length us, event | category | flops | bytes accessed | tf_op | source)
XLA Modules:
  0.0 148.1 jit_solution(14700330398085276428)
XLA Ops:
  0.0 1.9 %copy-done = bf16[3,2,1,64,4096]{4,3,2,1,0:T(8,128)(2,1)S(1)} copy-done((bf16[3,2,1,64,4096]{4,3,2,1,0:T(8,128)(2,1)S(1)}, bf16[3,2,1,64,4096]{4,3,2,1,0:T(8,128)(2,1)}, u32[]{:S(2)}) %copy-start) | copy-done | bytes 3145752
  1.9 1.1 copy_uv.1
  3.0 0.0 copy-start.9
  3.0 1.0 copy-done.9
  4.0 1.7 %collective-permute-start.1 = (bf16[1,2,64,4096]{3,2,1,0:T(8,128)(2,1)}, bf16[1,2,64,4096]{3,2,1,0:T(8,128)(2,1)}, u32[]{:S(2)}, u32[]{:S(2)}) collective-permute-start(bf16[1,2,64,4096]{3,2,1,0:T(8,128)(2,1)} %get-tuple-element.10), channel_id=1, source_target_pairs={{0,1},{1,0},{2,3},{3,2},{4,5},{5,4},{6,7},{7,6},{8,9},{9,8},{10,11... | collective-permute-start | bytes 3145736 | tf_op jit(solution)/shard_map/ppermute | solution.py:417
  5.7 3.2 %curl_x_2.1 = bf16[64,64,128]{2,1,0:T(8,128)(2,1)S(1)} custom-call(bf16[3,2,64,4096]{3,2,1,0:T(8,128)(2,1)S(1)} %bitcast.11, bf16[3,2,64,4096]{3,2,1,0:T(8,128)(2,1)S(1)} %bitcast.12, bf16[512,256]{1,0:T(8,128)(2,1)S(1)} %copy-done.5, f32[2,32,128]{2,1,0:T(8,128)S(1)} %copy-done.8), custom_call_target="tpu_custom_call" | custom-call | tf_op jit(solution)/shard_map/curl_x_2/pallas_call | solution.py:164
  8.9 1.0 copy-done.4
  9.9 11.4 %all-to-all-start.2 = ((bf16[64,64,128]{2,1,0:T(8,128)(2,1)}), bf16[64,64,128]{2,1,0:T(8,128)(2,1)}, u32[]{:S(2)}, u32[]{:S(2)}) async-start(bf16[64,64,128]{2,1,0:T(8,128)(2,1)} %copy-done.4), calls=%async_computation.2 | async-start | bytes 2097152 | tf_op jit(solution)/shard_map/all_to_all | solution.py:429
  21.3 0.2 collective-permute-start
  21.5 17.3 %collective-permute-done.1.refs_2_ = bf16[1,2,64,4096]{3,2,1,0:T(8,128)(2,1)} collective-permute-done((bf16[1,2,64,4096]{3,2,1,0:T(8,128)(2,1)}, bf16[1,2,64,4096]{3,2,1,0:T(8,128)(2,1)}, u32[]{:S(2)}, u32[]{:S(2)}) %collective-permute-start.1) | collective-permute-done | bytes 1048608 | tf_op jit(solution)/shard_map/ppermute | solution.py:417
  38.8 4.8 %curl_x_1.1 = bf16[64,64,128]{2,1,0:T(8,128)(2,1)S(1)} custom-call(bf16[3,2,64,4096]{3,2,1,0:T(8,128)(2,1)S(1)} %bitcast.13, bf16[3,2,64,4096]{3,2,1,0:T(8,128)(2,1)S(1)} %bitcast.14, bf16[1,2,64,4096]{3,2,1,0:T(8,128)(2,1)} %collective-permute-done.1.refs_2_, bf16[512,256]{1,0:T(8,128)(2,1)S(1)} %copy-done.5, f32[2,32,128]{2,1,0:T(8,128)S(1)} %copy-done.8), custom_call_target="tpu_custom_call" | custom-call | tf_op jit(solution)/shard_map/curl_x_1/pallas_call | solution.py:164
  43.6 0.0 copy-start.2
  43.6 1.0 copy-done.2
  44.6 2.1 %all-to-all-done.2.source = bf16[64,64,128]{2,1,0:T(8,128)(2,1)} async-done(((bf16[64,64,128]{2,1,0:T(8,128)(2,1)}), bf16[64,64,128]{2,1,0:T(8,128)(2,1)}, u32[]{:S(2)}, u32[]{:S(2)}) %all-to-all-start.2) | async-done | bytes 1048608 | tf_op jit(solution)/shard_map/all_to_all | solution.py:429
  46.7 9.6 %all-to-all-start.1 = ((bf16[64,64,128]{2,1,0:T(8,128)(2,1)}), bf16[64,64,128]{2,1,0:T(8,128)(2,1)}, u32[]{:S(2)}, u32[]{:S(2)}) async-start(bf16[64,64,128]{2,1,0:T(8,128)(2,1)} %copy-done.2), calls=%async_computation.1 | async-start | bytes 2097152 | tf_op jit(solution)/shard_map/all_to_all | solution.py:429
  56.4 16.1 %collective-permute-done.refs_2_ = bf16[1,2,64,4096]{3,2,1,0:T(8,128)(2,1)} collective-permute-done((bf16[1,2,64,4096]{3,2,1,0:T(8,128)(2,1)}, bf16[1,2,64,4096]{3,2,1,0:T(8,128)(2,1)}, u32[]{:S(2)}, u32[]{:S(2)}) %collective-permute-start) | collective-permute-done | bytes 1048608 | tf_op jit(solution)/shard_map/ppermute | solution.py:417
  72.5 4.8 %curl_x_0.1 = bf16[64,64,128]{2,1,0:T(8,128)(2,1)S(1)} custom-call(bf16[3,2,64,4096]{3,2,1,0:T(8,128)(2,1)S(1)} %bitcast.15, bf16[3,2,64,4096]{3,2,1,0:T(8,128)(2,1)S(1)} %bitcast.16, bf16[1,2,64,4096]{3,2,1,0:T(8,128)(2,1)} %collective-permute-done.refs_2_, bf16[512,256]{1,0:T(8,128)(2,1)S(1)} %copy-done.5, f32[2,32,128]{2,1,0:T(8,128)S(1)} %copy-done.8), custom_call_target="tpu_custom_call" | custom-call | tf_op jit(solution)/shard_map/curl_x_0/pallas_call | solution.py:164
  77.3 0.0 copy-start.3
  77.3 1.0 copy-done.3
  78.3 1.6 %all-to-all-done.1.source = bf16[64,64,128]{2,1,0:T(8,128)(2,1)} async-done(((bf16[64,64,128]{2,1,0:T(8,128)(2,1)}), bf16[64,64,128]{2,1,0:T(8,128)(2,1)}, u32[]{:S(2)}, u32[]{:S(2)}) %all-to-all-start.1) | async-done | bytes 1048608 | tf_op jit(solution)/shard_map/all_to_all | solution.py:429
  79.8 10.2 %all-to-all-start = ((bf16[64,64,128]{2,1,0:T(8,128)(2,1)}), bf16[64,64,128]{2,1,0:T(8,128)(2,1)S(1)}, u32[]{:S(2)}, u32[]{:S(2)}) async-start(bf16[64,64,128]{2,1,0:T(8,128)(2,1)} %copy-done.3), calls=%async_computation | async-start | bytes 2097152 | tf_op jit(solution)/shard_map/all_to_all | solution.py:429
  90.1 2.8 %y_first.1.before = f32[128,2048]{1,0:T(8,128)S(1)} custom-call(bf16[64,64,128]{2,1,0:T(8,128)(2,1)} %all-to-all-done.2.source, bf16[256,256]{1,0:T(8,128)(2,1)S(1)} %copy-done.6, f32[2,64,128]{2,1,0:T(8,128)S(1)} %copy-done.7), custom_call_target="tpu_custom_call" | custom-call | flops 268435456 | bytes 4194304 | tf_op jit(solution)/shard_map/y_first/pallas_call | solution.py:251
  92.9 2.8 %y_next.1.before = f32[128,2048]{1,0:T(8,128)S(1)} custom-call(bf16[64,64,128]{2,1,0:T(8,128)(2,1)} %all-to-all-done.1.source, f32[128,2048]{1,0:T(8,128)S(1)} %y_first.1.before, bf16[256,256]{1,0:T(8,128)(2,1)S(1)} %copy-done.6, f32[2,64,128]{2,1,0:T(8,128)S(1)} %copy-done.7), custom_call_target="tpu_custom_call" | custom-call | flops 268435456 | bytes 4194304 | tf_op jit(solution)/shard_map/y_next/pallas_call | solution.py:251
  95.7 14.0 %all-to-all-done.source = bf16[64,64,128]{2,1,0:T(8,128)(2,1)S(1)} async-done(((bf16[64,64,128]{2,1,0:T(8,128)(2,1)}), bf16[64,64,128]{2,1,0:T(8,128)(2,1)S(1)}, u32[]{:S(2)}, u32[]{:S(2)}) %all-to-all-start) | async-done | bytes 1048608 | tf_op jit(solution)/shard_map/all_to_all | solution.py:429
  109.8 1.7 %y_last.1 = bf16[8,32,2304]{2,1,0:T(8,128)(2,1)S(1)} custom-call(bf16[64,64,128]{2,1,0:T(8,128)(2,1)S(1)} %all-to-all-done.source, f32[128,2048]{1,0:T(8,128)S(1)} %y_next.1.before, bf16[256,256]{1,0:T(8,128)(2,1)S(1)} %copy-done.6, f32[2,64,128]{2,1,0:T(8,128)S(1)} %copy-done.7), custom_call_target="tpu_custom_call" | custom-call | flops 268435456 | bytes 4194304 | tf_op jit(solution)/shard_map/y_last/pallas_call | solution.py:251
  111.5 19.8 %all_to_all.20.field = bf16[8,32,2304]{2,1,0:T(8,128)(2,1)S(1)} all-to-all(bf16[8,32,2304]{2,1,0:T(8,128)(2,1)S(1)} %y_last.1), channel_id=1, replica_groups=mesh['row'=16,'col'=4,'gz'=2] {'gz','col'}, dimensions={0} | all-to-all | bytes 2359296 | tf_op jit(solution)/shard_map/all_to_all | solution.py:437
  131.4 0.7 collective-permute-start.3
  132.0 0.0 collective-permute-start.2
  132.1 2.0 %regroup.1 = (f32[72,16,256]{2,1,0:T(8,128)S(1)}, f32[72,16,256]{2,1,0:T(8,128)S(1)}) custom-call(bf16[8,32,2304]{2,1,0:T(8,128)(2,1)S(1)} %all_to_all.20.field), custom_call_target="tpu_custom_call" | custom-call | flops 16777216 | bytes 8388608 | tf_op jit(solution)/shard_map/regroup/pallas_call | solution.py:306
  134.0 0.7 collective-permute-done.3.high
  134.7 5.5 %collective-permute-done.2.low = bf16[2,16,2304]{2,1,0:T(8,128)(2,1)S(1)} collective-permute-done((bf16[2,16,2304]{2,1,0:T(8,128)(2,1)S(1)}, bf16[2,16,2304]{2,1,0:T(8,128)(2,1)S(1)}, u32[]{:S(2)}, u32[]{:S(2)}) %collective-permute-start.2) | collective-permute-done | bytes 147488 | tf_op jit(solution)/shard_map/ppermute | solution.py:417
  140.2 7.9 %smooth.1 = f32[1,1024,256]{2,1,0:T(8,128)} custom-call(f32[72,16,256]{2,1,0:T(8,128)S(1)} %get-tuple-element.11.own, f32[72,16,256]{2,1,0:T(8,128)S(1)} %get-tuple-element.12.other, bf16[2,16,2304]{2,1,0:T(8,128)(2,1)S(1)} %collective-permute-done.2.low, bf16[2,16,2304]{2,1,0:T(8,128)(2,1)S(1)} %collective-permute-done.3.high), custom_call_target="tpu_custom_call" | custom-call | tf_op jit(solution)/shard_map/smooth/pallas_call | solution.py:378
  (13 shorter events, 0.0 us)
Async XLA Ops:
  0.0 1.9 %copy-start = (bf16[3,2,1,64,4096]{4,3,2,1,0:T(8,128)(2,1)S(1)}, bf16[3,2,1,64,4096]{4,3,2,1,0:T(8,128)(2,1)}, u32[]{:S(2)}) copy-start(bf16[3,2,1,64,4096]{4,3,2,1,0:T(8,128)(2,1)} %param.5) | copy-start | bytes 9437188
  1.9 3.8 %copy-start.5 = (bf16[512,256]{1,0:T(8,128)(2,1)S(1)}, bf16[512,256]{1,0:T(8,128)(2,1)}, u32[]{:S(2)}) copy-start(bf16[512,256]{1,0:T(8,128)(2,1)} %constant.8.clone.refs_3_.refs_2_) | copy-start | bytes 786436
  1.9 3.8 %copy-start.8 = (f32[2,32,128]{2,1,0:T(8,128)S(1)}, f32[2,32,128]{2,1,0:T(8,128)}, u32[]{:S(2)}) copy-start(f32[2,32,128]{2,1,0:T(8,128)} %constant.9.clone.refs_4_.refs_3_) | copy-start | bytes 98308
  3.0 1.0 copy-start.9
  4.0 34.8 %collective-permute-start.1 = (bf16[1,2,64,4096]{3,2,1,0:T(8,128)(2,1)}, bf16[1,2,64,4096]{3,2,1,0:T(8,128)(2,1)}, u32[]{:S(2)}, u32[]{:S(2)}) collective-permute-start(bf16[1,2,64,4096]{3,2,1,0:T(8,128)(2,1)} %get-tuple-element.10), channel_id=1, source_target_pairs={{0,1},{1,0},{2,3},{3,2},{4,5},{5,4},{6,7},{7,6},{8,9},{9,8},{10,11... | collective-permute-start | bytes 3145736 | tf_op jit(solution)/shard_map/ppermute | solution.py:417
  5.7 33.1 %copy-start.1 = (bf16[3,2,1,64,4096]{4,3,2,1,0:T(8,128)(2,1)S(1)}, bf16[3,2,1,64,4096]{4,3,2,1,0:T(8,128)(2,1)}, u32[]{:S(2)}) copy-start(bf16[3,2,1,64,4096]{4,3,2,1,0:T(8,128)(2,1)} %param.5) | copy-start | bytes 9437188
  8.9 1.0 copy-start.4
  9.9 36.9 %all-to-all-start.2 = ((bf16[64,64,128]{2,1,0:T(8,128)(2,1)}), bf16[64,64,128]{2,1,0:T(8,128)(2,1)}, u32[]{:S(2)}, u32[]{:S(2)}) async-start(bf16[64,64,128]{2,1,0:T(8,128)(2,1)} %copy-done.4), calls=%async_computation.2 | async-start | bytes 2097152 | tf_op jit(solution)/shard_map/all_to_all | solution.py:429
  21.3 51.2 %collective-permute-start = (bf16[1,2,64,4096]{3,2,1,0:T(8,128)(2,1)}, bf16[1,2,64,4096]{3,2,1,0:T(8,128)(2,1)}, u32[]{:S(2)}, u32[]{:S(2)}) collective-permute-start(bf16[1,2,64,4096]{3,2,1,0:T(8,128)(2,1)} %copy-done.9), channel_id=1, source_target_pairs={{0,1},{1,0},{2,3},{3,2},{4,5},{5,4},{6,7},{7,6},{8,9},{9,8},{10,11... | collective-permute-start | bytes 3145736 | tf_op jit(solution)/shard_map/ppermute | solution.py:417
  43.6 1.0 copy-start.2
  46.7 33.1 %all-to-all-start.1 = ((bf16[64,64,128]{2,1,0:T(8,128)(2,1)}), bf16[64,64,128]{2,1,0:T(8,128)(2,1)}, u32[]{:S(2)}, u32[]{:S(2)}) async-start(bf16[64,64,128]{2,1,0:T(8,128)(2,1)} %copy-done.2), calls=%async_computation.1 | async-start | bytes 2097152 | tf_op jit(solution)/shard_map/all_to_all | solution.py:429
  77.3 1.0 copy-start.3
  78.3 11.8 %copy-start.6 = (bf16[256,256]{1,0:T(8,128)(2,1)S(1)}, bf16[256,256]{1,0:T(8,128)(2,1)}, u32[]{:S(2)}) copy-start(bf16[256,256]{1,0:T(8,128)(2,1)} %constant.10.clone.matrix) | copy-start | bytes 393220
  78.3 11.8 %copy-start.7 = (f32[2,64,128]{2,1,0:T(8,128)S(1)}, f32[2,64,128]{2,1,0:T(8,128)}, u32[]{:S(2)}) copy-start(f32[2,64,128]{2,1,0:T(8,128)} %constant.11.clone.twist) | copy-start | bytes 196612
  79.8 29.9 %all-to-all-start = ((bf16[64,64,128]{2,1,0:T(8,128)(2,1)}), bf16[64,64,128]{2,1,0:T(8,128)(2,1)S(1)}, u32[]{:S(2)}, u32[]{:S(2)}) async-start(bf16[64,64,128]{2,1,0:T(8,128)(2,1)} %copy-done.3), calls=%async_computation | async-start | bytes 2097152 | tf_op jit(solution)/shard_map/all_to_all | solution.py:429
  131.4 3.4 %collective-permute-start.3 = (bf16[2,16,2304]{2,1,0:T(8,128)(2,1)S(1)}, bf16[2,16,2304]{2,1,0:T(8,128)(2,1)S(1)}, u32[]{:S(2)}, u32[]{:S(2)}) collective-permute-start(bf16[2,16,2304]{2,1,0:T(8,128)(2,1)S(1)} %get-tuple-element.13), channel_id=1, source_target_pairs={{0,120},{8,0},{16,8},{24,16},{32,24},{40,32},{48,40},{56,48},{64,5... | collective-permute-start | bytes 442376 | tf_op jit(solution)/shard_map/ppermute | solution.py:417
  132.0 8.2 %collective-permute-start.2 = (bf16[2,16,2304]{2,1,0:T(8,128)(2,1)S(1)}, bf16[2,16,2304]{2,1,0:T(8,128)(2,1)S(1)}, u32[]{:S(2)}, u32[]{:S(2)}) collective-permute-start(bf16[2,16,2304]{2,1,0:T(8,128)(2,1)S(1)} %get-tuple-element.14), channel_id=1, source_target_pairs={{0,8},{8,16},{16,24},{24,32},{32,40},{40,48},{48,56},{56,64},{64,7... | collective-permute-start | bytes 442376 | tf_op jit(solution)/shard_map/ppermute | solution.py:417
